TPU v7x, 32 devices: a whole 2x2x4 slice. The times are simulated.
32 devices in a mesh: inst: 2 (over x), section: 2 (over core), tensor: 8 (over z, y).
Axes of the slice: x: 2, y: 2, z: 4, core: 2. Of those that a mesh axis runs over, the one named last changes fastest.
Arguments:
- queries: bfloat16 [2, 2, 8, 6, 1024], P('inst', 'section', 'tensor'), may hold values from -6 to 6
- resident_kv: bfloat16 [2, 2, 8, 2, 6, 2048, 256], P('inst', 'section', 'tensor'), may hold values from -6 to 6
- row_lengths: int32 [2, 6], P('inst'), may hold values from 2 to 2048, as said below
- out_weight: bfloat16 [2, 2, 8, 1024, 4096], P('inst', 'section', 'tensor'), may hold values from -0.5 to 0.5
- outgoing_kv: bfloat16 [2, 2, 8, 2, 256, 16, 256], P('inst', 'section', 'tensor'), may hold values from -6 to 6
- block_order: int32 [2, 2, 8, 256], P('inst', 'section', 'tensor'), may hold values from 0 to 255, each once within a row
- sent_length: int32 [2], P('inst'), may hold values from 1024 to 4096, as said below
Outputs:
- attn_out: float32 [2, 4, 6, 4096], P('inst', 'section', None, 'tensor')
- arrived_kv: bfloat16 [2, 2, 8, 2, 4096, 256], P('inst', 'section', 'tensor')
Inputs may be any that keep to these rules, and one draw needn't show every extreme that they name: `row_lengths`: some row of each instance attends 2048 positions. `sent_length`: one of the two instances sends 4096 valid positions, the other fewer. `block_order`: each device's list is a permutation of its 256 stored blocks.
All inputs are finite; a program needn't handle non-finite values.
Results may differ from a plain program's by a relative error of at most 0.005.
Values may be sent and summed in bfloat16 or wider, within the bound.
A program may use at most 128 MiB of HBM per device.

v0:
```python
import jax
import jax.numpy as jnp
from jax import lax
from jax.sharding import PartitionSpec as P

HEADS = 32
KV_HEADS = 8


def partner(x, axis, bit):
    return lax.ppermute(x, axis, [(i, i ^ 1 << bit) for i in range(lax.axis_size(axis))])


def passed_along(block, axis, distance):
    devices = range(lax.axis_size(axis))
    route = [((i - distance) % len(devices), i) for i in devices]
    return lax.ppermute(block, axis, route)


def pick_unit(pair_units, selector):
    return jnp.where(selector == 0, pair_units[0], pair_units[1])


def order_blocks(stored, block_ids, length):
    logical = jnp.take(stored, block_ids, axis=1)
    unit_count, block_count, block_len, lane_width = logical.shape
    logical = logical.reshape(unit_count, block_count * block_len, lane_width)
    positions = jnp.arange(block_count * block_len, dtype=jnp.int32)
    keep_mask = (positions < length)[None, :, None]
    return jnp.where(keep_mask, logical, jnp.zeros_like(logical))


def attend_slots(query_rows, cache_units, lengths, unit_of):
    row_count = query_rows.shape[0]
    head_dim = cache_units.shape[-1] // 2
    slot_count = query_rows.shape[1] // head_dim
    context = cache_units.shape[2]
    query_heads = query_rows.reshape(row_count, slot_count, head_dim)
    key_part = cache_units[..., :head_dim]
    value_part = cache_units[..., head_dim:]
    scores = jnp.einsum(
        "rkd,urcd->ukrc", query_heads, key_part, preferred_element_type=jnp.float32
    ) * head_dim ** (-0.5)
    first_unit = (unit_of == 0)[:, None, None]
    chosen = jnp.where(first_unit, scores[0], scores[1])
    live_mask = jnp.arange(context, dtype=jnp.int32)[None, :] < lengths[:, None]
    chosen = jnp.where(live_mask[None], chosen, -1e30)
    row_top = jnp.max(chosen, axis=2, keepdims=True)
    raised = jnp.exp(chosen - row_top)
    weights = (raised / jnp.sum(raised, axis=2, keepdims=True)).astype(jnp.bfloat16)
    mixture = jnp.einsum("krc,urcd->ukrd", weights, value_part, preferred_element_type=jnp.float32)
    head_out = jnp.where(first_unit, mixture[0], mixture[1]).astype(jnp.bfloat16)
    return jnp.transpose(head_out, (1, 0, 2)).reshape(row_count, slot_count * head_dim)


def project_layers(flat_heads, weight, layer_of, head_dim):
    lane_layer = jnp.repeat(layer_of, head_dim)
    blank = jnp.zeros_like(flat_heads)
    masked = jnp.stack(
        [jnp.where(lane_layer[None, :] == layer_pos, flat_heads, blank) for layer_pos in (0, 1)]
    )
    return jnp.einsum("jrs,sd->jrd", masked, weight, preferred_element_type=jnp.float32)


def per_device(
    queries, resident_kv, row_lengths, out_weight, outgoing_kv, block_order, sent_length
):
    second = lax.axis_index("inst") == 1
    parity = lax.axis_index("tensor") % 2
    query_rows = queries[0, 0, 0]
    cache_units = resident_kv[0, 0, 0]
    head_dim = cache_units.shape[-1] // 2
    slot_count = query_rows.shape[1] // head_dim
    per_layer = slot_count // 2
    group_size = HEADS // KV_HEADS
    paired = slot_count > group_size
    slot_ids = jnp.arange(slot_count, dtype=jnp.int32)
    unit_of = jnp.where(second, slot_ids // per_layer, slot_ids // group_size)
    layer_of = jnp.where(second, slot_ids // per_layer, parity)
    logical = order_blocks(outgoing_kv[0, 0, 0], block_order[0, 0, 0], sent_length[0])
    empty_unit = jnp.zeros_like(logical[0])
    if paired:
        own_unit = pick_unit(logical, parity)
        offered = pick_unit(logical, 1 - parity)
    else:
        own_unit = pick_unit(logical, jnp.where(second, parity, 0))
        offered = own_unit
    returned = partner(offered, "tensor", 0)
    ordered_pair = jnp.stack(
        [jnp.where(parity == 0, own_unit, returned), jnp.where(parity == 0, returned, own_unit)]
    )
    if paired:
        shipment = ordered_pair
    else:
        shipment = jnp.where(second, jnp.stack([own_unit, empty_unit]), ordered_pair)
    arrived = passed_along(shipment, "inst", 1)
    flat_heads = attend_slots(query_rows, cache_units, row_lengths[0], unit_of)
    partial_value = project_layers(flat_heads, out_weight[0, 0, 0], layer_of, head_dim)
    totals = lax.psum_scatter(partial_value, "tensor", scatter_dimension=2, tiled=True)
    return (totals[None], arrived[None, None, None])


def solution(mesh):
    placed = (
        P("inst", "section", "tensor", None, None),
        P("inst", "section", "tensor", None, None, None, None),
        P("inst", None),
        P("inst", "section", "tensor", None, None),
        P("inst", "section", "tensor", None, None, None, None),
        P("inst", "section", "tensor", None),
        P("inst"),
    )
    return jax.shard_map(
        per_device,
        mesh=mesh,
        in_specs=placed,
        out_specs=(
            P("inst", "section", None, "tensor"),
            P("inst", "section", "tensor", None, None, None),
        ),
        check_vma=False,
    )
```

profile of v0, /device:TPU:0, one launch (start us, length us, event | category | flops | bytes accessed | tf_op | source)
XLA Modules:
  0.0 183.6 jit_solution(18265465744687416007)
XLA Ops:
  7.2 0.0 reduce-scatter.2.cloned.1.call-start
  7.2 0.7 compare_select_fusion
  7.9 5.0 %gather_fusion = bf16[256,2,16,256]{3,2,1,0:T(8,128)(2,1)} fusion(bf16[2,256,16,256]{3,2,1,0:T(8,128)(2,1)} %bitcast.102, s32[1024]{0:T(1024)S(1)} %pad_clamp_fusion), kind=kCustom, calls=%fused_computation | custom fusion | bytes 8389632 | tf_op jit(solution)/shard_map/jit(_take)/gather | solution.py:25
  12.9 4.5 %copy.17 = bf16[2,256,16,256]{3,2,1,0:T(8,128)(2,1)} copy(bf16[2,256,16,256]{3,2,0,1:T(8,128)(2,1)} %bitcast.99) | data formatting | bytes 8388608 | tf_op jit(solution)/shard_map/jit(_take)/gather | solution.py:25
  17.4 0.0 copy-done.1
  17.4 0.1 broadcast_in_dim.102
  17.5 0.1 broadcast_in_dim.103
  18.3 5.3 %fusion.7 = bf16[2,4096,256]{2,1,0:T(8,128)(2,1)S(1)} fusion(bf16[2,256,16,256]{3,2,1,0:T(8,128)(2,1)} %copy.17, pred[4096]{0:T(1024)(128)(4,1)S(1)} %broadcast_in_dim.103, pred[4096]{0:T(1024)(128)(4,1)S(1)} %iota_compare_fusion.1), kind=kLoop, calls=%fused_computation.11 | loop fusion | flops 4194304 | bytes 8396800 | tf_op jit(solution)/shard_map/jit(_where)/select_n | solution.py:30
  23.6 0.0 copy-start
  23.6 2.0 %copy-done = bf16[2,4096,256]{2,1,0:T(8,128)(2,1)} copy-done((bf16[2,4096,256]{2,1,0:T(8,128)(2,1)}, bf16[2,4096,256]{2,1,0:T(8,128)(2,1)S(1)}, u32[]{:S(2)}) %copy-start) | copy-done | bytes 4194328
  25.6 0.2 select_bitcast_fusion
  25.8 3.0 %collective-permute-start = (bf16[4096,256]{1,0:T(8,128)(2,1)S(1)}, bf16[4096,256]{1,0:T(8,128)(2,1)}, u32[]{:S(2)}, u32[]{:S(2)}) collective-permute-start(bf16[4096,256]{1,0:T(8,128)(2,1)S(1)} %select_bitcast_fusion), channel_id=1, source_target_pairs={{0,1},{1,0},{2,3},{3,2},{4,5},{5,4},{6,7},{7,6},{8,9},{9,8},{10,11... | collective-permute-start | bytes 6291464 | tf_op jit(solution)/shard_map/ppermute | solution.py:11
  28.9 45.7 %collective-permute-done = bf16[4096,256]{1,0:T(8,128)(2,1)} collective-permute-done((bf16[4096,256]{1,0:T(8,128)(2,1)S(1)}, bf16[4096,256]{1,0:T(8,128)(2,1)}, u32[]{:S(2)}, u32[]{:S(2)}) %collective-permute-start) | collective-permute-done | bytes 2097184 | tf_op jit(solution)/shard_map/ppermute | solution.py:11
  74.6 3.2 %fusion.16 = (bf16[1,4096,256]{2,1,0:T(8,128)(2,1)S(1)}, bf16[1,4096,256]{2,1,0:T(8,128)(2,1)S(1)}) fusion(bf16[4096,256]{1,0:T(8,128)(2,1)} %collective-permute-done, pred[]{:T(512)S(6)} %eq.54, bf16[2,4096,256]{2,1,0:T(8,128)(2,1)} %copy-done), kind=kLoop, calls=%fused_computation.18 | loop fusion | flops 3145728 | bytes 10486784 | tf_op jit(solution)/shard_map/stack | solution.py:89
  77.8 2.4 %pad_maximum_fusion = bf16[2,4096,256]{2,1,0:T(8,128)(2,1)} fusion(bf16[1,4096,256]{2,1,0:T(8,128)(2,1)S(1)} %get-tuple-element.7, bf16[1,4096,256]{2,1,0:T(8,128)(2,1)S(1)} %get-tuple-element.6), kind=kLoop, calls=%fused_computation.9 | loop fusion | flops 2097152 | bytes 8388608 | tf_op jit(solution)/shard_map/stack | solution.py:89
  80.2 1.7 collective-permute-start.1
  81.9 6.1 %copy.29 = bf16[1,1,1,2,6,2048,256]{6,5,3,4,2,1,0:T(8,128)(2,1)S(1)} copy(bf16[1,1,1,2,6,2048,256]{6,5,4,3,2,1,0:T(8,128)(2,1)} %param.8) | data formatting | bytes 25165824 | tf_op args[1]
  88.0 0.0 copy-done.2
  88.1 0.1 iota_compare_fusion
  88.1 0.0 copy-done.3
  88.1 1.7 fusion.11
  89.9 0.4 fusion.35
  90.2 1.0 fusion.18
  91.2 0.1 fusion.29
  91.3 0.1 broadcast_bitcast_fusion.1
  91.4 0.1 broadcast_bitcast_fusion
  91.5 5.3 %fusion.1 = f32[2,6,4096]{2,1,0:T(8,128)} fusion(bf16[1,1,1,1024,4096]{4,3,2,1,0:T(8,128)(2,1)} %param.10, bf16[1,6,1024]{2,1,0:T(8,128)(2,1)S(1)} %get-tuple-element.9, bf16[1,6,1024]{2,1,0:T(8,128)(2,1)S(1)} %get-tuple-element.8), kind=kOutput, calls=%fused_computation.3 | convolution fusion | flops 100675584 | bytes 8609792 | tf_op jit(solution)/shard_map/jrs,sd->jrd/dot_general | solution.py:62
  96.9 0.0 reduce-scatter.2.cloned.1.call-update
  96.9 61.7 %reduce-scatter.2.cloned.1.call-done = f32[2,6,512]{2,1,0:T(8,128)} async-done(((f32[2,6,4096]{2,1,0:T(8,128)}), f32[2,6,512]{2,1,0:T(8,128)}) %reduce-scatter.2.cloned.1.call-update) | async-done | bytes 24592 | tf_op jit(solution)/shard_map/reduce_scatter | solution.py:99
  158.6 1.4 copy.18
  160.0 12.3 %collective-permute-done.1 = bf16[2,4096,256]{2,1,0:T(8,128)(2,1)} collective-permute-done((bf16[2,4096,256]{2,1,0:T(8,128)(2,1)}, bf16[2,4096,256]{2,1,0:T(8,128)(2,1)}, u32[]{:S(2)}, u32[]{:S(2)}) %collective-permute-start.1) | collective-permute-done | bytes 4194336 | tf_op jit(solution)/shard_map/ppermute | solution.py:17
  172.3 4.5 %copy.32 = bf16[1,1,1,2,4096,256]{5,4,3,2,1,0:T(8,128)(2,1)} copy(bf16[1,1,1,2,4096,256]{5,4,3,2,1,0:T(8,128)(2,1)} %bitcast.28) | data formatting | bytes 8388608
  (10 shorter events, 0.1 us)
Async XLA Ops:
  7.2 151.4 %reduce-scatter.2.cloned.1.call-start = ((), (), s32[]{:S(2)}) async-start(), calls=%async_computation.1 | async-start | bytes 294912 | tf_op jit(solution)/shard_map/reduce_scatter | solution.py:99
  12.9 4.5 %copy-start.1 = (s32[1,1,1,256]{3,2,1,0:T(1,128)S(1)}, s32[1,1,1,256]{3,2,1,0:T(1,128)}, u32[]{:S(2)}) copy-start(s32[1,1,1,256]{3,2,1,0:T(1,128)} %param.12) | copy-start | bytes 3076
  23.6 2.0 %copy-start = (bf16[2,4096,256]{2,1,0:T(8,128)(2,1)}, bf16[2,4096,256]{2,1,0:T(8,128)(2,1)S(1)}, u32[]{:S(2)}) copy-start(bf16[2,4096,256]{2,1,0:T(8,128)(2,1)S(1)} %fusion.7) | copy-start | bytes 12582916
  25.8 48.8 %collective-permute-start = (bf16[4096,256]{1,0:T(8,128)(2,1)S(1)}, bf16[4096,256]{1,0:T(8,128)(2,1)}, u32[]{:S(2)}, u32[]{:S(2)}) collective-permute-start(bf16[4096,256]{1,0:T(8,128)(2,1)S(1)} %select_bitcast_fusion), channel_id=1, source_target_pairs={{0,1},{1,0},{2,3},{3,2},{4,5},{5,4},{6,7},{7,6},{8,9},{9,8},{10,11... | collective-permute-start | bytes 6291464 | tf_op jit(solution)/shard_map/ppermute | solution.py:11
  80.2 7.8 %copy-start.2 = (s32[1,6]{1,0:T(1,128)S(1)}, s32[1,6]{1,0:T(1,128)}, u32[]{:S(2)}) copy-start(s32[1,6]{1,0:T(1,128)} %param.9) | copy-start | bytes 76
  80.2 7.9 %copy-start.3 = (bf16[1,1,1,6,1024]{4,3,2,1,0:T(8,128)(2,1)S(1)}, bf16[1,1,1,6,1024]{4,3,2,1,0:T(8,128)(2,1)}, u32[]{:S(2)}) copy-start(bf16[1,1,1,6,1024]{4,3,2,1,0:T(8,128)(2,1)} %param.7) | copy-start | bytes 36868
  80.2 92.1 %collective-permute-start.1 = (bf16[2,4096,256]{2,1,0:T(8,128)(2,1)}, bf16[2,4096,256]{2,1,0:T(8,128)(2,1)}, u32[]{:S(2)}, u32[]{:S(2)}) collective-permute-start(bf16[2,4096,256]{2,1,0:T(8,128)(2,1)} %pad_maximum_fusion), channel_id=1, source_target_pairs={{16,0},{0,16},{17,1},{1,17},{18,2},{2,18},{19,3},{3,19},{20,4},{4,... | collective-permute-start | bytes 12582920 | tf_op jit(solution)/shard_map/ppermute | solution.py:17
Sparse Core Ops, SparseCore 0:
  97.0 61.5 reduce-scatter.1
where the time goes:
time: 184 us
  waiting for transfers between devices  120 us (65%)
  local copies, waits for them, and re-layouts  23.9 us (13%)
  between operations  14.8 us (8%)
  other arithmetic  12.3 us (7%)
  matrix products  8.04 us (4%)
  starting transfers between devices  4.78 us (3%)
    reduce_scatter x1, waiting for transfers between devices, per_device(): lax.psum_scatter(partial_value, 'tensor', scatter_dimension=2, tiled=True)  61.7 us
    ppermute x1, waiting for transfers between devices, partner(): lax.ppermute(x, axis, [(i, i ^ 1 << bit) for i in range(lax.axis_size(axi...  45.7 us
    unnamed x11, local copies, waits for them, and re-layouts  14 us
    ppermute x1, waiting for transfers between devices, passed_along(): return lax.ppermute(block, axis, route)  12.3 us
    gather x2, local copies, waits for them, and re-layouts, order_blocks(): logical = jnp.take(stored, block_ids, axis=1)  9.49 us
    another operation x2, other arithmetic, per_device(): jnp.stack([jnp.where(parity == 0, own_unit, returned), jnp.where(parity =...  5.6 us
    dot_general x1, matrix products, project_layers(): jnp.einsum('jrs,sd->jrd', masked, weight, preferred_element_type=jnp.floa...  5.34 us
    select_n x1, other arithmetic, order_blocks(): return jnp.where(keep_mask, logical, jnp.zeros_like(logical))  5.26 us
  transfers between devices with their start and end apart: 3, of which 3 were waited for; matrix products, arithmetic and copies ran while one was open for 9% of the time, Pallas kernels for 0%

commit v1 on v0

v1 whole, which is shorter than its diff:
```python
import functools

import jax
import jax.numpy as jnp
from jax import lax
from jax.experimental import pallas as pl
from jax.experimental.pallas import tpu as pltpu
from jax.sharding import PartitionSpec as P

HEADS = 32
KV_HEADS = 8
SHARES = (1, 3, 4, 4, 3, 1)


def halved_sum(value, axis):
    size = lax.axis_size(axis)
    place = lax.axis_index(axis)
    bit = size.bit_length() - 2
    while bit >= 0:
        step = 1 << bit
        half = value.shape[-1] // 2
        side = (place // step) % 2
        kept = lax.dynamic_slice_in_dim(value, side * half, half, value.ndim - 1)
        given = lax.dynamic_slice_in_dim(value, (1 - side) * half, half, value.ndim - 1)
        value = kept + lax.ppermute(given, axis, [(i, i ^ step) for i in range(size)])
        bit -= 1
    return value


def sent_units(paired):
    parity = lax.axis_index("tensor") % 2
    if paired:
        return parity, 1 - parity
    return lax.axis_index("inst") * parity, 0 * parity


def order_kernel(starts, paired, order_ref, length_ref, stored_ref, *rest):
    chunk_refs, (edge, blank, edge_sem, sem) = rest[:-4], rest[-4:]
    block_len = edge.shape[1]
    units = sent_units(paired)
    length = length_ref[0]
    full = length // block_len
    blank[...] = jnp.zeros_like(blank)

    for part, start in enumerate(starts):
        count = chunk_refs[2 * part].shape[0] // block_len
        whole = jnp.clip(full - start, 0, count)

        def copy_block(i, carry):
            stored_at = order_ref[start + i]
            for way in range(2):
                pltpu.make_async_copy(
                    stored_ref.at[units[way], stored_at],
                    chunk_refs[2 * part + way].at[pl.ds(i * block_len, block_len)],
                    sem,
                ).start()
            return carry

        def blank_block(i, carry):
            for way in range(2):
                pltpu.make_async_copy(
                    blank, chunk_refs[2 * part + way].at[pl.ds(i * block_len, block_len)], sem
                ).start()
            return carry

        lax.fori_loop(0, whole, copy_block, 0)
        here = (full >= start) & (full < start + count)

        @pl.when(here)
        def _():
            stored_at = order_ref[full]
            for way in range(2):
                fetch = pltpu.make_async_copy(
                    stored_ref.at[units[way], stored_at], edge.at[way], edge_sem
                )
                fetch.start()
                fetch.wait()
            rows = lax.broadcasted_iota(jnp.int32, edge.shape, 1)
            edge[...] = jnp.where(
                rows < length - full * block_len, edge[...].astype(jnp.float32), 0.0
            ).astype(edge.dtype)
            for way in range(2):
                pltpu.make_async_copy(
                    edge.at[way],
                    chunk_refs[2 * part + way].at[pl.ds((full - start) * block_len, block_len)],
                    sem,
                ).start()

        lax.fori_loop(whole + here.astype(jnp.int32), count, blank_block, 0)

    for chunk_ref in chunk_refs:
        pltpu.make_async_copy(chunk_ref, chunk_ref, sem).wait()


def first_kernel(paired, order_ref, stored_ref, same_ref, other_ref, sem):
    block_len = stored_ref.shape[2]
    units = sent_units(paired)
    for i in range(same_ref.shape[0] // block_len):
        for unit, chunk_ref in zip(units, (same_ref, other_ref)):
            pltpu.make_async_copy(
                stored_ref.at[unit, order_ref[i]], chunk_ref.at[pl.ds(i * block_len, block_len)], sem
            ).start()
    for chunk_ref in (same_ref, other_ref):
        pltpu.make_async_copy(chunk_ref, chunk_ref, sem).wait()


def first_chunks(stored, block_ids, paired, count):
    block_len, lane_width = stored.shape[2:]
    chunk_shape = jax.ShapeDtypeStruct((count * block_len, lane_width), stored.dtype)
    return pl.pallas_call(
        functools.partial(first_kernel, paired),
        out_shape=[chunk_shape] * 2,
        in_specs=[
            pl.BlockSpec(memory_space=pltpu.SMEM),
            pl.BlockSpec(memory_space=pltpu.HBM),
        ],
        out_specs=[pl.BlockSpec(memory_space=pltpu.HBM)] * 2,
        scratch_shapes=[pltpu.SemaphoreType.DMA],
        compiler_params=pltpu.CompilerParams(vmem_limit_bytes=60 * 1024 * 1024),
    )(block_ids, stored)


def room_kernel(out_ref):
    pass


def room(shape, dtype):
    return pl.pallas_call(
        room_kernel,
        out_shape=jax.ShapeDtypeStruct(shape, dtype),
        out_specs=pl.BlockSpec(memory_space=pltpu.HBM),
    )()


def ordered_chunks(stored, block_ids, sent_length, paired, starts, counts):
    block_len, lane_width = stored.shape[2:]
    chunk_shapes = []
    for count in counts:
        chunk_shapes += [jax.ShapeDtypeStruct((count * block_len, lane_width), stored.dtype)] * 2
    total = sum(counts) * block_len * lane_width * 2
    return pl.pallas_call(
        functools.partial(order_kernel, starts, paired),
        out_shape=chunk_shapes,
        in_specs=[
            pl.BlockSpec(memory_space=pltpu.SMEM),
            pl.BlockSpec(memory_space=pltpu.SMEM),
            pl.BlockSpec(memory_space=pltpu.HBM),
        ],
        out_specs=[pl.BlockSpec(memory_space=pltpu.HBM)] * len(chunk_shapes),
        scratch_shapes=[
            pltpu.VMEM((2, block_len, lane_width), stored.dtype),
            pltpu.VMEM((block_len, lane_width), stored.dtype),
            pltpu.SemaphoreType.DMA,
            pltpu.SemaphoreType.DMA,
        ],
        compiler_params=pltpu.CompilerParams(vmem_limit_bytes=48 * 1024 * 1024),
        cost_estimate=pl.CostEstimate(flops=0, bytes_accessed=4 * total, transcendentals=0),
    )(block_ids, sent_length, stored)


def cuts(block_count):
    unit = block_count // 16
    counts = [share * unit for share in SHARES]
    starts = [sum(counts[:i]) for i in range(len(counts))]
    return starts, counts


def crossed(chunk, flip, both):
    size = lax.axis_size("tensor")
    route = [(t, size + (t ^ flip)) for t in range(size)]
    if both:
        route += [(size + t, t ^ flip) for t in range(size)]
    return lax.ppermute(chunk, ("inst", "tensor"), route)


def attend_kernel(group_size, lengths_ref, query_ref, keys_ref, values_ref, out_ref):
    unit, row = pl.program_id(0), pl.program_id(1)
    slot_count, head_dim = query_ref.shape[1:]
    context = keys_ref.shape[0]
    scores = lax.dot_general(
        query_ref[row], keys_ref[...], (((1,), (1,)), ((), ())), preferred_element_type=jnp.float32
    ) * head_dim ** (-0.5)
    positions = lax.broadcasted_iota(jnp.int32, (slot_count, context), 1)
    scores = jnp.where(positions < lengths_ref[0, row], scores, -1e30)
    raised = jnp.exp(scores - jnp.max(scores, axis=1, keepdims=True))
    weights = (raised / jnp.sum(raised, axis=1, keepdims=True)).astype(jnp.bfloat16)
    mixture = jnp.dot(weights, values_ref[...], preferred_element_type=jnp.float32)
    slot_ids = lax.broadcasted_iota(jnp.int32, (slot_count, head_dim), 0)
    second = lax.axis_index("inst") == 1
    beyond = jnp.where(second, slot_count // 2, group_size)
    mine = (slot_ids >= beyond) == (unit == 1)

    @pl.when(unit == 0)
    def _():
        out_ref[row] = mixture

    @pl.when(unit == 1)
    def _():
        out_ref[row] = jnp.where(mine, mixture, out_ref[row])


def attend_slots(query_rows, cache_units, lengths):
    row_count = query_rows.shape[0]
    unit_count, _, context, lane_width = cache_units.shape
    head_dim = lane_width // 2
    slot_count = query_rows.shape[1] // head_dim
    query_heads = query_rows.reshape(row_count, slot_count, head_dim)
    mixture = pl.pallas_call(
        functools.partial(attend_kernel, HEADS // KV_HEADS),
        grid=(unit_count, row_count),
        out_shape=jax.ShapeDtypeStruct((row_count, slot_count, head_dim), jnp.float32),
        in_specs=[
            pl.BlockSpec(memory_space=pltpu.SMEM),
            pl.BlockSpec((row_count, slot_count, head_dim), lambda u, r: (0, 0, 0)),
            pl.BlockSpec((None, None, context, head_dim), lambda u, r: (u, r, 0, 0)),
            pl.BlockSpec((None, None, context, head_dim), lambda u, r: (u, r, 0, 1)),
        ],
        out_specs=pl.BlockSpec((row_count, slot_count, head_dim), lambda u, r: (0, 0, 0)),
        cost_estimate=pl.CostEstimate(
            flops=4 * cache_units.size * slot_count // 2,
            bytes_accessed=2 * cache_units.size,
            transcendentals=unit_count * row_count * slot_count * context,
        ),
        compiler_params=pltpu.CompilerParams(vmem_limit_bytes=32 * 1024 * 1024),
    )(lengths, query_heads, cache_units, cache_units)
    return mixture.astype(jnp.bfloat16).reshape(row_count, slot_count * head_dim)


def project_layers(flat_heads, weight, layer_of, head_dim):
    lane_layer = jnp.repeat(layer_of, head_dim)
    blank = jnp.zeros_like(flat_heads)
    masked = jnp.stack(
        [jnp.where(lane_layer[None, :] == layer_pos, flat_heads, blank) for layer_pos in (0, 1)]
    )
    return jnp.einsum("jrs,sd->jrd", masked, weight, preferred_element_type=jnp.float32)


def per_device(
    queries, resident_kv, row_lengths, out_weight, outgoing_kv, block_order, sent_length
):
    second = lax.axis_index("inst") == 1
    parity = lax.axis_index("tensor") % 2
    query_rows = queries[0, 0, 0]
    cache_units = resident_kv[0, 0, 0]
    head_dim = cache_units.shape[-1] // 2
    slot_count = query_rows.shape[1] // head_dim
    per_layer = slot_count // 2
    group_size = HEADS // KV_HEADS
    paired = slot_count > group_size
    slot_ids = jnp.arange(slot_count, dtype=jnp.int32)
    layer_of = jnp.where(second, slot_ids // per_layer, parity)
    stored = outgoing_kv[0, 0, 0]
    unit_count, block_count, block_len, lane_width = stored.shape
    block_ids = block_order[0, 0, 0]
    starts, counts = cuts(block_count)
    chunks = list(first_chunks(stored, block_ids, paired, counts[0]))
    chunks += ordered_chunks(stored, block_ids, sent_length, paired, starts[1:], counts[1:])
    if paired:
        same_slot, other_slot = parity, 1 - parity
    else:
        same_slot = jnp.where(second, parity, 0)
        other_slot = jnp.where(second, 1 - parity, 1)
    arrived = room((unit_count, block_count * block_len, lane_width), stored.dtype)
    landed = [None] * len(chunks)

    def send(parts):
        for part in parts:
            landed[2 * part] = crossed(chunks[2 * part], 0, True)
            landed[2 * part + 1] = crossed(chunks[2 * part + 1], 1, paired)

    early = len(counts) - 2
    send(range(early))
    query_rows, cache_units, landed[2], landed[3] = lax.optimization_barrier(
        (query_rows, cache_units, landed[2], landed[3])
    )
    flat_heads = attend_slots(query_rows, cache_units, row_lengths)
    partial_value = project_layers(flat_heads, out_weight[0, 0, 0], layer_of, head_dim)
    totals = halved_sum(partial_value, "tensor")
    totals, *chunks[2 * early :] = lax.optimization_barrier((totals, *chunks[2 * early :]))
    send(range(early, len(counts)))
    for part, start in enumerate(starts):
        for way, slot in enumerate((same_slot, other_slot)):
            place = (slot, start * block_len, 0)
            arrived = lax.dynamic_update_slice(arrived, landed[2 * part + way][None], place)
    return (totals[None], arrived[None, None, None])


def solution(mesh):
    placed = (
        P("inst", "section", "tensor", None, None),
        P("inst", "section", "tensor", None, None, None, None),
        P("inst", None),
        P("inst", "section", "tensor", None, None),
        P("inst", "section", "tensor", None, None, None, None),
        P("inst", "section", "tensor", None),
        P("inst"),
    )
    return jax.shard_map(
        per_device,
        mesh=mesh,
        in_specs=placed,
        out_specs=(
            P("inst", "section", None, "tensor"),
            P("inst", "section", "tensor", None, None, None),
        ),
        check_vma=False,
    )
```

time: 184 us -> 117 us (0.64)
  waiting for transfers between devices: 120 us -> 28.4 us
  Pallas kernels: 0 us -> 33.4 us
  starting transfers between devices: 4.78 us -> 25.1 us
  between operations: 14.8 us -> 1.41 us
  other arithmetic: 12.3 us -> 0.06 us
  matrix products: 8.04 us -> 4.64 us
    reduce_scatter x1 -> x0, waiting for transfers between devices: 61.7 us -> none  [per_device(): lax.psum_scatter(partial_value, 'tensor', scatter_dimension=2, tiled=True)]
    pallas_call x0 -> x4, Pallas kernels: none -> 33.4 us  [the longest x1 13.6 us: ordered_chunks(): pl.pallas_call(functools.partial(order_kernel, starts, paired), out_shape...]
    ppermute x2 -> x15, waiting for transfers between devices: 58 us -> 28.4 us  [the longest x12 20.9 us: crossed(): return lax.ppermute(chunk, ('inst', 'tensor'), route)]
    ppermute x2 -> x15, starting transfers between devices: 4.74 us -> 25.1 us  [the longest x12 17.4 us: crossed(): return lax.ppermute(chunk, ('inst', 'tensor'), route)]
    dynamic_update_slice x0 -> x12, local copies, waits for them, and re-layouts: none -> 17 us  [per_device(): lax.dynamic_update_slice(arrived, landed[2 * part + way][None], place)]
    gather x2 -> x0, local copies, waits for them, and re-layouts: 9.49 us -> none  [order_blocks(): logical = jnp.take(stored, block_ids, axis=1)]
    unnamed x11 -> x8, local copies, waits for them, and re-layouts: 14 us -> 5.93 us
    select_n x3 -> x0, other arithmetic: 6.16 us -> none  [the longest x1 5.26 us: order_blocks(): return jnp.where(keep_mask, logical, jnp.zeros_like(logical))]
  transfers between devices with their start and end apart: 3 -> 15, of which waited for: 3 -> 8; matrix products, arithmetic and copies ran while one was open for 9% -> 19% of each run, Pallas kernels for 0% -> 20%
where the time goes in v1:
time: 117 us; the launch traced here: 116 us
  Pallas kernels  33.4 us (29%)
  waiting for transfers between devices  28.4 us (24%)
  starting transfers between devices  25.1 us (21%)
  local copies, waits for them, and re-layouts  23.2 us (20%)
  matrix products  4.64 us (4%)
  between operations  1.41 us (1%)
    ppermute x12, waiting for transfers between devices, crossed(): return lax.ppermute(chunk, ('inst', 'tensor'), route)  20.9 us
    ppermute x12, starting transfers between devices, crossed(): return lax.ppermute(chunk, ('inst', 'tensor'), route)  17.4 us
    dynamic_update_slice x12, local copies, waits for them, and re-layouts, per_device(): lax.dynamic_update_slice(arrived, landed[2 * part + way][None], place)  17 us
    pallas_call x1, Pallas kernels, ordered_chunks(): pl.pallas_call(functools.partial(order_kernel, starts, paired), out_shape...  13.6 us
    pallas_call x1, Pallas kernels, attend_slots(): pl.pallas_call(functools.partial(attend_kernel, HEADS // KV_HEADS), grid=...  9.9 us
    pallas_call x1, Pallas kernels, first_chunks(): pl.pallas_call(functools.partial(first_kernel, paired), out_shape=[chunk_...  9.89 us
    ppermute x3, starting transfers between devices, halved_sum(): lax.ppermute(given, axis, [(i, i ^ step) for i in range(size)])  7.74 us
    ppermute x3, waiting for transfers between devices, halved_sum(): lax.ppermute(given, axis, [(i, i ^ step) for i in range(size)])  7.51 us
  transfers between devices with their start and end apart: 15, of which 8 were waited for; matrix products, arithmetic and copies ran while one was open for 19% of the time, Pallas kernels for 20%

profile of v1, /device:TPU:0, one launch (start us, length us, event | category | flops | bytes accessed | tf_op | source)
XLA Modules:
  0.0 116.2 jit_solution(1468826020850910898)
XLA Ops:
  0.6 9.9 %shard_map.89 = (bf16[256,256]{1,0:T(8,128)(2,1)}, bf16[256,256]{1,0:T(8,128)(2,1)}) custom-call(s32[256]{0:T(256)} %bitcast.46, bf16[2,256,16,256]{3,2,1,0:T(8,128)(2,1)} %bitcast.48), custom_call_target="tpu_custom_call" | custom-call | tf_op jit(solution)/shard_map/pallas_call | solution.py:110
  10.5 3.0 %collective-permute-start.5 = (bf16[256,256]{1,0:T(8,128)(2,1)}, bf16[256,256]{1,0:T(8,128)(2,1)}, u32[]{:S(2)}, u32[]{:S(2)}) collective-permute-start(bf16[256,256]{1,0:T(8,128)(2,1)} %get-tuple-element.32), channel_id=1, source_target_pairs={{0,16},{1,17},{2,18},{3,19},{4,20},{5,21},{6,22},{7,23},{16,0},{17... | collective-permute-start | bytes 393224 | tf_op jit(solution)/shard_map/ppermute | solution.py:173
  13.5 1.5 %collective-permute-start.6 = (bf16[256,256]{1,0:T(8,128)(2,1)}, bf16[256,256]{1,0:T(8,128)(2,1)}, u32[]{:S(2)}, u32[]{:S(2)}) collective-permute-start(bf16[256,256]{1,0:T(8,128)(2,1)} %get-tuple-element.33), channel_id=1, source_target_pairs={{0,17},{1,16},{2,19},{3,18},{4,21},{5,20},{6,23},{7,22},{16,1},{17... | collective-permute-start | bytes 393224 | tf_op jit(solution)/shard_map/ppermute | solution.py:173
  15.7 13.6 %shard_map.86 = (bf16[768,256]{1,0:T(8,128)(2,1)}, bf16[768,256]{1,0:T(8,128)(2,1)S(1)}, bf16[1024,256]{1,0:T(8,128)(2,1)S(1)}, bf16[1024,256]{1,0:T(8,128)(2,1)...) custom-call(s32[256]{0:T(256)S(1)} %bitcast.47, ...), custom_call_target="tpu_custom_call" | custom-call | bytes 7864320 | tf_op jit(solution)/shard_map/pallas_call | solution.py:141
  29.3 1.6 %collective-permute-start = (bf16[768,256]{1,0:T(8,128)(2,1)}, bf16[768,256]{1,0:T(8,128)(2,1)}, u32[]{:S(2)}, u32[]{:S(2)}) collective-permute-start(bf16[768,256]{1,0:T(8,128)(2,1)} %get-tuple-element.23), channel_id=1, source_target_pairs={{0,16},{1,17},{2,18},{3,19},{4,20},{5,21},{6,22},{7,23},{16,0},{17... | collective-permute-start | bytes 1179656 | tf_op jit(solution)/shard_map/ppermute | solution.py:173
  30.9 1.9 %collective-permute-start.7 = (bf16[1024,256]{1,0:T(8,128)(2,1)S(1)}, bf16[1024,256]{1,0:T(8,128)(2,1)}, u32[]{:S(2)}, u32[]{:S(2)}) collective-permute-start(bf16[1024,256]{1,0:T(8,128)(2,1)S(1)} %get-tuple-element.36), channel_id=1, source_target_pairs={{0,16},{1,17},{2,18},{3,19},{4,20},{5,21},{6,22},{7,23},{16,0},{17... | collective-permute-start | bytes 1572872 | tf_op jit(solution)/shard_map/ppermute | solution.py:173
  33.0 1.5 %collective-permute-start.8 = (bf16[1024,256]{1,0:T(8,128)(2,1)S(1)}, bf16[1024,256]{1,0:T(8,128)(2,1)}, u32[]{:S(2)}, u32[]{:S(2)}) collective-permute-start(bf16[1024,256]{1,0:T(8,128)(2,1)S(1)} %get-tuple-element.37), channel_id=1, source_target_pairs={{0,17},{1,16},{2,19},{3,18},{4,21},{5,20},{6,23},{7,22},{16,1},{17... | collective-permute-start | bytes 1572872 | tf_op jit(solution)/shard_map/ppermute | solution.py:173
  34.5 1.6 %bitcast_dynamic-update-slice_fusion.11 = bf16[1,1,1,2,4096,256]{5,4,3,2,1,0:T(8,128)(2,1)} fusion(bf16[1,1,1,2,4096,256]{5,4,3,2,1,0:T(8,128)(2,1)} %bitcast.50, s32[]{:T(128)S(6)} %select_n.109, bf16[256,256]{1,0:T(8,128)(2,1)} %collective-permute-done.5), kind=kLoop, calls=%fused_computation.13 | loop fusion | bytes 262148 | tf_op jit(solution)/shard_map/dynamic_update_slice | solution.py:284
  36.1 1.5 %collective-permute-start.9 = (bf16[1024,256]{1,0:T(8,128)(2,1)S(1)}, bf16[1024,256]{1,0:T(8,128)(2,1)}, u32[]{:S(2)}, u32[]{:S(2)}) collective-permute-start(bf16[1024,256]{1,0:T(8,128)(2,1)S(1)} %get-tuple-element.38), channel_id=1, source_target_pairs={{0,16},{1,17},{2,18},{3,19},{4,20},{5,21},{6,22},{7,23},{16,0},{17... | collective-permute-start | bytes 1572872 | tf_op jit(solution)/shard_map/ppermute | solution.py:173
  37.6 1.6 %bitcast_dynamic-update-slice_fusion.10 = bf16[1,1,1,2,4096,256]{5,4,3,2,1,0:T(8,128)(2,1)} fusion(bf16[1,1,1,2,4096,256]{5,4,3,2,1,0:T(8,128)(2,1)} %bitcast_dynamic-update-slice_fusion.11, s32[]{:T(128)S(6)} %select_n.110, bf16[256,256]{1,0:T(8,128)(2,1)} %collective-permute-done.6), kind=kLoop, calls=%fused_computation.12 | loop fusion | bytes 262148 | tf_op jit(solution)/shard_map/dynamic_update_slice | solution.py:284
  39.1 2.6 %collective-permute-done = bf16[768,256]{1,0:T(8,128)(2,1)} collective-permute-done((bf16[768,256]{1,0:T(8,128)(2,1)}, bf16[768,256]{1,0:T(8,128)(2,1)}, u32[]{:S(2)}, u32[]{:S(2)}) %collective-permute-start) | collective-permute-done | bytes 393248 | tf_op jit(solution)/shard_map/ppermute | solution.py:173
  41.8 1.4 %collective-permute-start.10 = (bf16[1024,256]{1,0:T(8,128)(2,1)S(1)}, bf16[1024,256]{1,0:T(8,128)(2,1)}, u32[]{:S(2)}, u32[]{:S(2)}) collective-permute-start(bf16[1024,256]{1,0:T(8,128)(2,1)S(1)} %get-tuple-element.39), channel_id=1, source_target_pairs={{0,17},{1,16},{2,19},{3,18},{4,21},{5,20},{6,23},{7,22},{16,1},{17... | collective-permute-start | bytes 1572872 | tf_op jit(solution)/shard_map/ppermute | solution.py:173
  43.2 6.5 %collective-permute-done.1 = bf16[768,256]{1,0:T(8,128)(2,1)} collective-permute-done((bf16[768,256]{1,0:T(8,128)(2,1)S(1)}, bf16[768,256]{1,0:T(8,128)(2,1)}, u32[]{:S(2)}, u32[]{:S(2)}) %collective-permute-start.1) | collective-permute-done | bytes 393248 | tf_op jit(solution)/shard_map/ppermute | solution.py:173
  50.4 4.6 %copy-done = bf16[1,1,1,2,6,2048,256]{6,5,4,3,2,1,0:T(8,128)(2,1)S(1)} copy-done((bf16[1,1,1,2,6,2048,256]{6,5,4,3,2,1,0:T(8,128)(2,1)S(1)}, bf16[1,1,1,2,6,2048,256]{6,5,4,3,2,1,0:T(8,128)(2,1)}, u32[]{:S(2)}) %copy-start) | copy-done | bytes 12582936
  55.0 9.9 %shard_map.87 = f32[6,8,128]{2,1,0:T(8,128)S(1)} custom-call(s32[1,6]{1,0:T(1,128)S(1)} %copy-done.2, bf16[6,8,128]{2,1,0:T(8,128)(2,1)S(1)} %bitcast.45, bf16[2,6,2048,256]{3,2,1,0:T(8,128)(2,1)S(1)} %bitcast.43, bf16[2,6,2048,256]{3,2,1,0:T(8,128)(2,1)S(1)} %bitcast.44), custom_call_target="tpu_custom_call" | custom-call | flops 100663296 | bytes 12582912 | tf_op jit(solution)/shard_map/pallas_call | solution.py:208
  65.0 4.6 %fusion = f32[2,6,4096]{2,1,0:T(8,128)S(1)} fusion(bf16[1,1,1,1024,4096]{4,3,2,1,0:T(8,128)(2,1)} %param.10, bf16[1,6,1024]{2,1,0:T(8,128)(2,1)S(1)} %get-tuple-element.47, bf16[1,6,1024]{2,1,0:T(8,128)(2,1)S(1)} %get-tuple-element.46), kind=kOutput, calls=%fused_computation | convolution fusion | flops 100675584 | bytes 8609792 | tf_op jit(solution)/shard_map/jrs,sd->jrd/dot_general | solution.py:235
  69.6 3.1 %collective-permute-start.2 = (f32[2,6,2048]{2,1,0:T(8,128)S(1)}, f32[2,6,2048]{2,1,0:T(8,128)S(1)}, u32[]{:S(2)}, u32[]{:S(2)}) collective-permute-start(f32[2,6,2048]{2,1,0:T(8,128)S(1)} %constant_dynamic-slice_fusion.2), channel_id=1, source_target_pairs={{0,4},{1,5},{2,6},{3,7},{4,0},{5,1},{6,2},{7,3},{8,12},{9,13},{10,... | collective-permute-start | bytes 294920 | tf_op jit(solution)/shard_map/ppermute | solution.py:25
  72.7 1.8 %bitcast_dynamic-update-slice_fusion.7 = bf16[1,1,1,2,4096,256]{5,4,3,2,1,0:T(8,128)(2,1)} fusion(bf16[1,1,1,2,4096,256]{5,4,3,2,1,0:T(8,128)(2,1)} %bitcast_dynamic-update-slice_fusion.10, s32[]{:T(128)S(6)} %select_n.109, bf16[768,256]{1,0:T(8,128)(2,1)} %collective-permute-done), kind=kLoop, calls=%fused_computation.9 | loop fusion | bytes 786436 | tf_op jit(solution)/shard_map/dynamic_update_slice | solution.py:284
  74.5 1.8 %bitcast_dynamic-update-slice_fusion.6 = bf16[1,1,1,2,4096,256]{5,4,3,2,1,0:T(8,128)(2,1)} fusion(bf16[1,1,1,2,4096,256]{5,4,3,2,1,0:T(8,128)(2,1)} %bitcast_dynamic-update-slice_fusion.7, s32[]{:T(128)S(6)} %select_n.110, bf16[768,256]{1,0:T(8,128)(2,1)} %collective-permute-done.1), kind=kLoop, calls=%fused_computation.8 | loop fusion | bytes 786436 | tf_op jit(solution)/shard_map/dynamic_update_slice | solution.py:284
  76.3 1.9 %collective-permute-start.3 = (f32[2,6,1024]{2,1,0:T(8,128)S(1)}, f32[2,6,1024]{2,1,0:T(8,128)S(1)}, u32[]{:S(2)}, u32[]{:S(2)}) collective-permute-start(f32[2,6,1024]{2,1,0:T(8,128)S(1)} %constant_dynamic-slice_fusion.1), channel_id=1, source_target_pairs={{0,2},{1,3},{2,0},{3,1},{4,6},{5,7},{6,4},{7,5},{8,10},{9,11},{10,... | collective-permute-start | bytes 147464 | tf_op jit(solution)/shard_map/ppermute | solution.py:25
  78.2 1.9 %bitcast_dynamic-update-slice_fusion.3 = bf16[1,1,1,2,4096,256]{5,4,3,2,1,0:T(8,128)(2,1)} fusion(bf16[1,1,1,2,4096,256]{5,4,3,2,1,0:T(8,128)(2,1)} %bitcast_dynamic-update-slice_fusion.6, s32[]{:T(128)S(6)} %select_n.109, bf16[1024,256]{1,0:T(8,128)(2,1)} %collective-permute-done.7), kind=kLoop, calls=%fused_computation.5 | loop fusion | bytes 1048580 | tf_op jit(solution)/shard_map/dynamic_update_slice | solution.py:284
  80.7 2.7 %collective-permute-start.4 = (f32[2,6,512]{2,1,0:T(8,128)S(1)}, f32[2,6,512]{2,1,0:T(8,128)S(1)}, u32[]{:S(2)}, u32[]{:S(2)}) collective-permute-start(f32[2,6,512]{2,1,0:T(8,128)S(1)} %constant_dynamic-slice_fusion), channel_id=1, source_target_pairs={{0,1},{1,0},{2,3},{3,2},{4,5},{5,4},{6,7},{7,6},{8,9},{9,8},{10,11... | collective-permute-start | bytes 73736 | tf_op jit(solution)/shard_map/ppermute | solution.py:25
  83.4 1.9 %bitcast_dynamic-update-slice_fusion.2 = bf16[1,1,1,2,4096,256]{5,4,3,2,1,0:T(8,128)(2,1)} fusion(bf16[1,1,1,2,4096,256]{5,4,3,2,1,0:T(8,128)(2,1)} %bitcast_dynamic-update-slice_fusion.3, s32[]{:T(128)S(6)} %select_n.110, bf16[1024,256]{1,0:T(8,128)(2,1)} %collective-permute-done.8), kind=kLoop, calls=%fused_computation.4 | loop fusion | bytes 1048580 | tf_op jit(solution)/shard_map/dynamic_update_slice | solution.py:284
  85.3 6.9 %collective-permute-done.4 = f32[2,6,512]{2,1,0:T(8,128)S(1)} collective-permute-done((f32[2,6,512]{2,1,0:T(8,128)S(1)}, f32[2,6,512]{2,1,0:T(8,128)S(1)}, u32[]{:S(2)}, u32[]{:S(2)}) %collective-permute-start.4) | collective-permute-done | bytes 24608 | tf_op jit(solution)/shard_map/ppermute | solution.py:25
  92.2 1.4 %collective-permute-start.11 = (bf16[768,256]{1,0:T(8,128)(2,1)S(1)}, bf16[768,256]{1,0:T(8,128)(2,1)S(1)}, u32[]{:S(2)}, u32[]{:S(2)}) collective-permute-start(bf16[768,256]{1,0:T(8,128)(2,1)S(1)} %get-tuple-element.40), channel_id=1, source_target_pairs={{0,16},{1,17},{2,18},{3,19},{4,20},{5,21},{6,22},{7,23},{16,0},{17... | collective-permute-start | bytes 1179656 | tf_op jit(solution)/shard_map/ppermute | solution.py:173
  93.6 1.9 %bitcast_dynamic-update-slice_fusion.1 = bf16[1,1,1,2,4096,256]{5,4,3,2,1,0:T(8,128)(2,1)} fusion(bf16[1,1,1,2,4096,256]{5,4,3,2,1,0:T(8,128)(2,1)} %bitcast_dynamic-update-slice_fusion.2, s32[]{:T(128)S(6)} %select_n.109, bf16[1024,256]{1,0:T(8,128)(2,1)} %collective-permute-done.9), kind=kLoop, calls=%fused_computation.3 | loop fusion | bytes 1048580 | tf_op jit(solution)/shard_map/dynamic_update_slice | solution.py:284
  95.5 1.5 %collective-permute-start.12 = (bf16[768,256]{1,0:T(8,128)(2,1)S(1)}, bf16[768,256]{1,0:T(8,128)(2,1)S(1)}, u32[]{:S(2)}, u32[]{:S(2)}) collective-permute-start(bf16[768,256]{1,0:T(8,128)(2,1)S(1)} %get-tuple-element.41), channel_id=1, source_target_pairs={{0,17},{1,16},{2,19},{3,18},{4,21},{5,20},{6,23},{7,22},{16,1},{17... | collective-permute-start | bytes 1179656 | tf_op jit(solution)/shard_map/ppermute | solution.py:173
  97.0 1.9 %bitcast_dynamic-update-slice_fusion = bf16[1,1,1,2,4096,256]{5,4,3,2,1,0:T(8,128)(2,1)} fusion(bf16[1,1,1,2,4096,256]{5,4,3,2,1,0:T(8,128)(2,1)} %bitcast_dynamic-update-slice_fusion.1, s32[]{:T(128)S(6)} %select_n.110, bf16[1024,256]{1,0:T(8,128)(2,1)} %collective-permute-done.10), kind=kLoop, calls=%fused_computation.2 | loop fusion | bytes 1048580 | tf_op jit(solution)/shard_map/dynamic_update_slice | solution.py:284
  98.8 1.5 %collective-permute-start.13 = (bf16[256,256]{1,0:T(8,128)(2,1)S(1)}, bf16[256,256]{1,0:T(8,128)(2,1)S(1)}, u32[]{:S(2)}, u32[]{:S(2)}) collective-permute-start(bf16[256,256]{1,0:T(8,128)(2,1)S(1)} %get-tuple-element.42), channel_id=1, source_target_pairs={{0,16},{1,17},{2,18},{3,19},{4,20},{5,21},{6,22},{7,23},{16,0},{17... | collective-permute-start | bytes 393224 | tf_op jit(solution)/shard_map/ppermute | solution.py:173
  101.6 2.7 %collective-permute-done.11 = bf16[768,256]{1,0:T(8,128)(2,1)S(1)} collective-permute-done((bf16[768,256]{1,0:T(8,128)(2,1)S(1)}, bf16[768,256]{1,0:T(8,128)(2,1)S(1)}, u32[]{:S(2)}, u32[]{:S(2)}) %collective-permute-start.11) | collective-permute-done | bytes 393248 | tf_op jit(solution)/shard_map/ppermute | solution.py:173
  105.1 7.7 %collective-permute-done.12 = bf16[768,256]{1,0:T(8,128)(2,1)S(1)} collective-permute-done((bf16[768,256]{1,0:T(8,128)(2,1)S(1)}, bf16[768,256]{1,0:T(8,128)(2,1)S(1)}, u32[]{:S(2)}, u32[]{:S(2)}) %collective-permute-start.12) | collective-permute-done | bytes 393248 | tf_op jit(solution)/shard_map/ppermute | solution.py:173
  113.5 0.9 collective-permute-done.13
  (35 shorter events, 6.2 us)
Async XLA Ops:
  0.6 15.1 %copy-start.1 = (s32[1,1,1,256]{3,2,1,0:T(1,128)S(1)}, s32[1,1,1,256]{3,2,1,0:T(1,128)}, u32[]{:S(2)}) copy-start(s32[1,1,1,256]{3,2,1,0:T(1,128)} %param.12) | copy-start | bytes 3076
  10.5 22.5 %collective-permute-start.5 = (bf16[256,256]{1,0:T(8,128)(2,1)}, bf16[256,256]{1,0:T(8,128)(2,1)}, u32[]{:S(2)}, u32[]{:S(2)}) collective-permute-start(bf16[256,256]{1,0:T(8,128)(2,1)} %get-tuple-element.32), channel_id=1, source_target_pairs={{0,16},{1,17},{2,18},{3,19},{4,20},{5,21},{6,22},{7,23},{16,0},{17... | collective-permute-start | bytes 393224 | tf_op jit(solution)/shard_map/ppermute | solution.py:173
  13.5 22.6 %collective-permute-start.6 = (bf16[256,256]{1,0:T(8,128)(2,1)}, bf16[256,256]{1,0:T(8,128)(2,1)}, u32[]{:S(2)}, u32[]{:S(2)}) collective-permute-start(bf16[256,256]{1,0:T(8,128)(2,1)} %get-tuple-element.33), channel_id=1, source_target_pairs={{0,17},{1,16},{2,19},{3,18},{4,21},{5,20},{6,23},{7,22},{16,1},{17... | collective-permute-start | bytes 393224 | tf_op jit(solution)/shard_map/ppermute | solution.py:173
  15.7 34.7 %copy-start.2 = (s32[1,6]{1,0:T(1,128)S(1)}, s32[1,6]{1,0:T(1,128)}, u32[]{:S(2)}) copy-start(s32[1,6]{1,0:T(1,128)} %lengths_ref.1) | copy-start | bytes 76
  29.3 12.4 %collective-permute-start = (bf16[768,256]{1,0:T(8,128)(2,1)}, bf16[768,256]{1,0:T(8,128)(2,1)}, u32[]{:S(2)}, u32[]{:S(2)}) collective-permute-start(bf16[768,256]{1,0:T(8,128)(2,1)} %get-tuple-element.23), channel_id=1, source_target_pairs={{0,16},{1,17},{2,18},{3,19},{4,20},{5,21},{6,22},{7,23},{16,0},{17... | collective-permute-start | bytes 1179656 | tf_op jit(solution)/shard_map/ppermute | solution.py:173
  30.9 18.8 %collective-permute-start.1 = (bf16[768,256]{1,0:T(8,128)(2,1)S(1)}, bf16[768,256]{1,0:T(8,128)(2,1)}, u32[]{:S(2)}, u32[]{:S(2)}) collective-permute-start(bf16[768,256]{1,0:T(8,128)(2,1)S(1)} %get-tuple-element.24), channel_id=1, source_target_pairs={{0,17},{1,16},{2,19},{3,18},{4,21},{5,20},{6,23},{7,22},{16,1},{17... | collective-permute-start | bytes 1179656 | tf_op jit(solution)/shard_map/ppermute | solution.py:173
  30.9 47.3 %collective-permute-start.7 = (bf16[1024,256]{1,0:T(8,128)(2,1)S(1)}, bf16[1024,256]{1,0:T(8,128)(2,1)}, u32[]{:S(2)}, u32[]{:S(2)}) collective-permute-start(bf16[1024,256]{1,0:T(8,128)(2,1)S(1)} %get-tuple-element.36), channel_id=1, source_target_pairs={{0,16},{1,17},{2,18},{3,19},{4,20},{5,21},{6,22},{7,23},{16,0},{17... | collective-permute-start | bytes 1572872 | tf_op jit(solution)/shard_map/ppermute | solution.py:173
  33.0 50.4 %collective-permute-start.8 = (bf16[1024,256]{1,0:T(8,128)(2,1)S(1)}, bf16[1024,256]{1,0:T(8,128)(2,1)}, u32[]{:S(2)}, u32[]{:S(2)}) collective-permute-start(bf16[1024,256]{1,0:T(8,128)(2,1)S(1)} %get-tuple-element.37), channel_id=1, source_target_pairs={{0,17},{1,16},{2,19},{3,18},{4,21},{5,20},{6,23},{7,22},{16,1},{17... | collective-permute-start | bytes 1572872 | tf_op jit(solution)/shard_map/ppermute | solution.py:173
  36.1 57.5 %collective-permute-start.9 = (bf16[1024,256]{1,0:T(8,128)(2,1)S(1)}, bf16[1024,256]{1,0:T(8,128)(2,1)}, u32[]{:S(2)}, u32[]{:S(2)}) collective-permute-start(bf16[1024,256]{1,0:T(8,128)(2,1)S(1)} %get-tuple-element.38), channel_id=1, source_target_pairs={{0,16},{1,17},{2,18},{3,19},{4,20},{5,21},{6,22},{7,23},{16,0},{17... | collective-permute-start | bytes 1572872 | tf_op jit(solution)/shard_map/ppermute | solution.py:173
  41.8 55.2 %collective-permute-start.10 = (bf16[1024,256]{1,0:T(8,128)(2,1)S(1)}, bf16[1024,256]{1,0:T(8,128)(2,1)}, u32[]{:S(2)}, u32[]{:S(2)}) collective-permute-start(bf16[1024,256]{1,0:T(8,128)(2,1)S(1)} %get-tuple-element.39), channel_id=1, source_target_pairs={{0,17},{1,16},{2,19},{3,18},{4,21},{5,20},{6,23},{7,22},{16,1},{17... | collective-permute-start | bytes 1572872 | tf_op jit(solution)/shard_map/ppermute | solution.py:173
  50.4 4.6 %copy-start = (bf16[1,1,1,2,6,2048,256]{6,5,4,3,2,1,0:T(8,128)(2,1)S(1)}, bf16[1,1,1,2,6,2048,256]{6,5,4,3,2,1,0:T(8,128)(2,1)}, u32[]{:S(2)}) copy-start(bf16[1,1,1,2,6,2048,256]{6,5,4,3,2,1,0:T(8,128)(2,1)} %param.8) | copy-start | bytes 37748740
  69.6 6.7 %collective-permute-start.2 = (f32[2,6,2048]{2,1,0:T(8,128)S(1)}, f32[2,6,2048]{2,1,0:T(8,128)S(1)}, u32[]{:S(2)}, u32[]{:S(2)}) collective-permute-start(f32[2,6,2048]{2,1,0:T(8,128)S(1)} %constant_dynamic-slice_fusion.2), channel_id=1, source_target_pairs={{0,4},{1,5},{2,6},{3,7},{4,0},{5,1},{6,2},{7,3},{8,12},{9,13},{10,... | collective-permute-start | bytes 294920 | tf_op jit(solution)/shard_map/ppermute | solution.py:25
  76.3 4.3 %collective-permute-start.3 = (f32[2,6,1024]{2,1,0:T(8,128)S(1)}, f32[2,6,1024]{2,1,0:T(8,128)S(1)}, u32[]{:S(2)}, u32[]{:S(2)}) collective-permute-start(f32[2,6,1024]{2,1,0:T(8,128)S(1)} %constant_dynamic-slice_fusion.1), channel_id=1, source_target_pairs={{0,2},{1,3},{2,0},{3,1},{4,6},{5,7},{6,4},{7,5},{8,10},{9,11},{10,... | collective-permute-start | bytes 147464 | tf_op jit(solution)/shard_map/ppermute | solution.py:25
  80.7 11.5 %collective-permute-start.4 = (f32[2,6,512]{2,1,0:T(8,128)S(1)}, f32[2,6,512]{2,1,0:T(8,128)S(1)}, u32[]{:S(2)}, u32[]{:S(2)}) collective-permute-start(f32[2,6,512]{2,1,0:T(8,128)S(1)} %constant_dynamic-slice_fusion), channel_id=1, source_target_pairs={{0,1},{1,0},{2,3},{3,2},{4,5},{5,4},{6,7},{7,6},{8,9},{9,8},{10,11... | collective-permute-start | bytes 73736 | tf_op jit(solution)/shard_map/ppermute | solution.py:25
  92.2 12.1 %collective-permute-start.11 = (bf16[768,256]{1,0:T(8,128)(2,1)S(1)}, bf16[768,256]{1,0:T(8,128)(2,1)S(1)}, u32[]{:S(2)}, u32[]{:S(2)}) collective-permute-start(bf16[768,256]{1,0:T(8,128)(2,1)S(1)} %get-tuple-element.40), channel_id=1, source_target_pairs={{0,16},{1,17},{2,18},{3,19},{4,20},{5,21},{6,22},{7,23},{16,0},{17... | collective-permute-start | bytes 1179656 | tf_op jit(solution)/shard_map/ppermute | solution.py:173
  95.5 17.3 %collective-permute-start.12 = (bf16[768,256]{1,0:T(8,128)(2,1)S(1)}, bf16[768,256]{1,0:T(8,128)(2,1)S(1)}, u32[]{:S(2)}, u32[]{:S(2)}) collective-permute-start(bf16[768,256]{1,0:T(8,128)(2,1)S(1)} %get-tuple-element.41), channel_id=1, source_target_pairs={{0,17},{1,16},{2,19},{3,18},{4,21},{5,20},{6,23},{7,22},{16,1},{17... | collective-permute-start | bytes 1179656 | tf_op jit(solution)/shard_map/ppermute | solution.py:173
  98.8 15.5 %collective-permute-start.13 = (bf16[256,256]{1,0:T(8,128)(2,1)S(1)}, bf16[256,256]{1,0:T(8,128)(2,1)S(1)}, u32[]{:S(2)}, u32[]{:S(2)}) collective-permute-start(bf16[256,256]{1,0:T(8,128)(2,1)S(1)} %get-tuple-element.42), channel_id=1, source_target_pairs={{0,16},{1,17},{2,18},{3,19},{4,20},{5,21},{6,22},{7,23},{16,0},{17... | collective-permute-start | bytes 393224 | tf_op jit(solution)/shard_map/ppermute | solution.py:173
  100.3 15.2 %collective-permute-start.14 = (bf16[256,256]{1,0:T(8,128)(2,1)S(1)}, bf16[256,256]{1,0:T(8,128)(2,1)S(1)}, u32[]{:S(2)}, u32[]{:S(2)}) collective-permute-start(bf16[256,256]{1,0:T(8,128)(2,1)S(1)} %get-tuple-element.43), channel_id=1, source_target_pairs={{0,17},{1,16},{2,19},{3,18},{4,21},{5,20},{6,23},{7,22},{16,1},{17... | collective-permute-start | bytes 393224 | tf_op jit(solution)/shard_map/ppermute | solution.py:173

commit v2 on v1

--- a/solution.py
+++ b/solution.py
@@ -9,7 +9,7 @@
 
 HEADS = 32
 KV_HEADS = 8
-SHARES = (1, 3, 4, 4, 3, 1)
+SHARES = (3, 6, 8, 8, 6, 1)
 
 
 def halved_sum(value, axis):
@@ -35,12 +35,20 @@
 
 
 def order_kernel(starts, paired, order_ref, length_ref, stored_ref, *rest):
-    chunk_refs, (edge, blank, edge_sem, sem) = rest[:-4], rest[-4:]
+    chunk_refs, (held, edge, blank, edge_sem, sem) = rest[:-5], rest[-5:]
     block_len = edge.shape[1]
     units = sent_units(paired)
+    fetches = []
+    for way in range(2):
+        fetches.append(
+            pltpu.make_async_copy(stored_ref.at[units[way]], held.at[way], edge_sem.at[way])
+        )
+        fetches[way].start()
     length = length_ref[0]
     full = length // block_len
     blank[...] = jnp.zeros_like(blank)
+    for fetch in fetches:
+        fetch.wait()
 
     for part, start in enumerate(starts):
         count = chunk_refs[2 * part].shape[0] // block_len
@@ -50,7 +58,7 @@
             stored_at = order_ref[start + i]
             for way in range(2):
                 pltpu.make_async_copy(
-                    stored_ref.at[units[way], stored_at],
+                    held.at[way, stored_at],
                     chunk_refs[2 * part + way].at[pl.ds(i * block_len, block_len)],
                     sem,
                 ).start()
@@ -69,15 +77,9 @@
         @pl.when(here)
         def _():
             stored_at = order_ref[full]
-            for way in range(2):
-                fetch = pltpu.make_async_copy(
-                    stored_ref.at[units[way], stored_at], edge.at[way], edge_sem
-                )
-                fetch.start()
-                fetch.wait()
             rows = lax.broadcasted_iota(jnp.int32, edge.shape, 1)
             edge[...] = jnp.where(
-                rows < length - full * block_len, edge[...].astype(jnp.float32), 0.0
+                rows < length - full * block_len, held[:, stored_at].astype(jnp.float32), 0.0
             ).astype(edge.dtype)
             for way in range(2):
                 pltpu.make_async_copy(
@@ -114,7 +116,7 @@
             pl.BlockSpec(memory_space=pltpu.SMEM),
             pl.BlockSpec(memory_space=pltpu.HBM),
         ],
-        out_specs=[pl.BlockSpec(memory_space=pltpu.HBM)] * 2,
+        out_specs=[pl.BlockSpec(memory_space=pltpu.VMEM)] * 2,
         scratch_shapes=[pltpu.SemaphoreType.DMA],
         compiler_params=pltpu.CompilerParams(vmem_limit_bytes=60 * 1024 * 1024),
     )(block_ids, stored)
@@ -148,9 +150,10 @@
         ],
         out_specs=[pl.BlockSpec(memory_space=pltpu.HBM)] * len(chunk_shapes),
         scratch_shapes=[
+            pltpu.VMEM((2,) + stored.shape[1:], stored.dtype),
             pltpu.VMEM((2, block_len, lane_width), stored.dtype),
             pltpu.VMEM((block_len, lane_width), stored.dtype),
-            pltpu.SemaphoreType.DMA,
+            pltpu.SemaphoreType.DMA((2,)),
             pltpu.SemaphoreType.DMA,
         ],
         compiler_params=pltpu.CompilerParams(vmem_limit_bytes=48 * 1024 * 1024),
@@ -159,7 +162,7 @@
 
 
 def cuts(block_count):
-    unit = block_count // 16
+    unit = block_count // 32
     counts = [share * unit for share in SHARES]
     starts = [sum(counts[:i]) for i in range(len(counts))]
     return starts, counts

time: 117 us -> 103 us (0.88)
  Pallas kernels: 33.4 us -> 21.5 us
  starting transfers between devices: 25.1 us -> 23.5 us
    pallas_call x1, Pallas kernels: 9.89 us -> 2.58 us  [first_chunks(): pl.pallas_call(functools.partial(first_kernel, paired), out_shape=[chunk_...]
    pallas_call x1, Pallas kernels: 13.6 us -> 8.98 us  [ordered_chunks(): pl.pallas_call(functools.partial(order_kernel, starts, paired), out_shape...]
    ppermute x12, waiting for transfers between devices: 20.9 us -> 17.4 us  [crossed(): return lax.ppermute(chunk, ('inst', 'tensor'), route)]
    ppermute x3, waiting for transfers between devices: 7.51 us -> 10.8 us  [halved_sum(): lax.ppermute(given, axis, [(i, i ^ step) for i in range(size)])]
    ppermute x3, starting transfers between devices: 7.74 us -> 5.16 us  [halved_sum(): lax.ppermute(given, axis, [(i, i ^ step) for i in range(size)])]
    unnamed x8 -> x10, local copies, waits for them, and re-layouts: 5.93 us -> 5.22 us
  transfers between devices with their start and end apart: 15 -> 15, of which waited for: 8 -> 7; matrix products, arithmetic and copies ran while one was open for 19% -> 22% of each run, Pallas kernels for 20% -> 19%
where the time goes in v2:
time: 103 us; the launch traced here: 102 us
  waiting for transfers between devices  28.2 us (27%)
  starting transfers between devices  23.5 us (23%)
  local copies, waits for them, and re-layouts  22.5 us (22%)
  Pallas kernels  21.5 us (21%)
  matrix products  4.64 us (5%)
  between operations  1.43 us (1%)
    ppermute x12, starting transfers between devices, crossed(): return lax.ppermute(chunk, ('inst', 'tensor'), route)  18.4 us
    ppermute x12, waiting for transfers between devices, crossed(): return lax.ppermute(chunk, ('inst', 'tensor'), route)  17.4 us
    dynamic_update_slice x12, local copies, waits for them, and re-layouts, per_device(): lax.dynamic_update_slice(arrived, landed[2 * part + way][None], place)  17 us
    ppermute x3, waiting for transfers between devices, halved_sum(): lax.ppermute(given, axis, [(i, i ^ step) for i in range(size)])  10.8 us
    pallas_call x1, Pallas kernels, attend_slots(): pl.pallas_call(functools.partial(attend_kernel, HEADS // KV_HEADS), grid=...  9.9 us
    pallas_call x1, Pallas kernels, ordered_chunks(): pl.pallas_call(functools.partial(order_kernel, starts, paired), out_shape...  8.98 us
    unnamed x10, local copies, waits for them, and re-layouts  5.22 us
    ppermute x3, starting transfers between devices, halved_sum(): lax.ppermute(given, axis, [(i, i ^ step) for i in range(size)])  5.16 us
  transfers between devices with their start and end apart: 15, of which 7 were waited for; matrix products, arithmetic and copies ran while one was open for 22% of the time, Pallas kernels for 19%

profile of v2, /device:TPU:0, one launch (start us, length us, event | category | flops | bytes accessed | tf_op | source)
XLA Modules:
  0.0 101.9 jit_solution(3680227568915112355)
XLA Ops:
  0.6 2.6 %shard_map.89 = (bf16[384,256]{1,0:T(8,128)(2,1)}, bf16[384,256]{1,0:T(8,128)(2,1)}) custom-call(s32[256]{0:T(256)} %bitcast.46, bf16[2,256,16,256]{3,2,1,0:T(8,128)(2,1)} %bitcast.48), custom_call_target="tpu_custom_call" | custom-call | tf_op jit(solution)/shard_map/pallas_call | solution.py:112
  3.2 3.0 %collective-permute-start.5 = (bf16[384,256]{1,0:T(8,128)(2,1)}, bf16[384,256]{1,0:T(8,128)(2,1)}, u32[]{:S(2)}, u32[]{:S(2)}) collective-permute-start(bf16[384,256]{1,0:T(8,128)(2,1)} %get-tuple-element.32), channel_id=1, source_target_pairs={{0,16},{1,17},{2,18},{3,19},{4,20},{5,21},{6,22},{7,23},{16,0},{17... | collective-permute-start | bytes 589832 | tf_op jit(solution)/shard_map/ppermute | solution.py:176
  6.2 1.5 %collective-permute-start.6 = (bf16[384,256]{1,0:T(8,128)(2,1)}, bf16[384,256]{1,0:T(8,128)(2,1)}, u32[]{:S(2)}, u32[]{:S(2)}) collective-permute-start(bf16[384,256]{1,0:T(8,128)(2,1)} %get-tuple-element.33), channel_id=1, source_target_pairs={{0,17},{1,16},{2,19},{3,18},{4,21},{5,20},{6,23},{7,22},{16,1},{17... | collective-permute-start | bytes 589832 | tf_op jit(solution)/shard_map/ppermute | solution.py:176
  8.4 9.0 %shard_map.86 = (bf16[768,256]{1,0:T(8,128)(2,1)}, bf16[768,256]{1,0:T(8,128)(2,1)S(1)}, bf16[1024,256]{1,0:T(8,128)(2,1)S(1)}, bf16[1024,256]{1,0:T(8,128)(2,1)...) custom-call(s32[256]{0:T(256)S(1)} %bitcast.47, ...), custom_call_target="tpu_custom_call" | custom-call | bytes 7602176 | tf_op jit(solution)/shard_map/pallas_call | solution.py:143
  17.4 2.1 %collective-permute-start = (bf16[768,256]{1,0:T(8,128)(2,1)}, bf16[768,256]{1,0:T(8,128)(2,1)}, u32[]{:S(2)}, u32[]{:S(2)}) collective-permute-start(bf16[768,256]{1,0:T(8,128)(2,1)} %get-tuple-element.23), channel_id=1, source_target_pairs={{0,16},{1,17},{2,18},{3,19},{4,20},{5,21},{6,22},{7,23},{16,0},{17... | collective-permute-start | bytes 1179656 | tf_op jit(solution)/shard_map/ppermute | solution.py:176
  19.5 1.9 %collective-permute-start.7 = (bf16[1024,256]{1,0:T(8,128)(2,1)S(1)}, bf16[1024,256]{1,0:T(8,128)(2,1)}, u32[]{:S(2)}, u32[]{:S(2)}) collective-permute-start(bf16[1024,256]{1,0:T(8,128)(2,1)S(1)} %get-tuple-element.36), channel_id=1, source_target_pairs={{0,16},{1,17},{2,18},{3,19},{4,20},{5,21},{6,22},{7,23},{16,0},{17... | collective-permute-start | bytes 1572872 | tf_op jit(solution)/shard_map/ppermute | solution.py:176
  21.6 1.0 %collective-permute-start.8 = (bf16[1024,256]{1,0:T(8,128)(2,1)S(1)}, bf16[1024,256]{1,0:T(8,128)(2,1)}, u32[]{:S(2)}, u32[]{:S(2)}) collective-permute-start(bf16[1024,256]{1,0:T(8,128)(2,1)S(1)} %get-tuple-element.37), channel_id=1, source_target_pairs={{0,17},{1,16},{2,19},{3,18},{4,21},{5,20},{6,23},{7,22},{16,1},{17... | collective-permute-start | bytes 1572872 | tf_op jit(solution)/shard_map/ppermute | solution.py:176
  22.6 1.6 %bitcast_dynamic-update-slice_fusion.9 = bf16[1,1,1,2,4096,256]{5,4,3,2,1,0:T(8,128)(2,1)} fusion(bf16[1,1,1,2,4096,256]{5,4,3,2,1,0:T(8,128)(2,1)} %bitcast.50, s32[]{:T(128)S(6)} %select_n.109, bf16[384,256]{1,0:T(8,128)(2,1)} %collective-permute-done.5), kind=kLoop, calls=%fused_computation.11 | loop fusion | bytes 393220 | tf_op jit(solution)/shard_map/dynamic_update_slice | solution.py:287
  24.2 1.9 %collective-permute-start.9 = (bf16[1024,256]{1,0:T(8,128)(2,1)S(1)}, bf16[1024,256]{1,0:T(8,128)(2,1)}, u32[]{:S(2)}, u32[]{:S(2)}) collective-permute-start(bf16[1024,256]{1,0:T(8,128)(2,1)S(1)} %get-tuple-element.38), channel_id=1, source_target_pairs={{0,16},{1,17},{2,18},{3,19},{4,20},{5,21},{6,22},{7,23},{16,0},{17... | collective-permute-start | bytes 1572872 | tf_op jit(solution)/shard_map/ppermute | solution.py:176
  26.2 1.6 %bitcast_dynamic-update-slice_fusion.8 = bf16[1,1,1,2,4096,256]{5,4,3,2,1,0:T(8,128)(2,1)} fusion(bf16[1,1,1,2,4096,256]{5,4,3,2,1,0:T(8,128)(2,1)} %bitcast_dynamic-update-slice_fusion.9, s32[]{:T(128)S(6)} %select_n.110, bf16[384,256]{1,0:T(8,128)(2,1)} %collective-permute-done.6), kind=kLoop, calls=%fused_computation.10 | loop fusion | bytes 393220 | tf_op jit(solution)/shard_map/dynamic_update_slice | solution.py:287
  27.8 2.0 %collective-permute-done = bf16[768,256]{1,0:T(8,128)(2,1)} collective-permute-done((bf16[768,256]{1,0:T(8,128)(2,1)}, bf16[768,256]{1,0:T(8,128)(2,1)}, u32[]{:S(2)}, u32[]{:S(2)}) %collective-permute-start) | collective-permute-done | bytes 393248 | tf_op jit(solution)/shard_map/ppermute | solution.py:176
  29.8 1.9 %collective-permute-start.10 = (bf16[1024,256]{1,0:T(8,128)(2,1)S(1)}, bf16[1024,256]{1,0:T(8,128)(2,1)}, u32[]{:S(2)}, u32[]{:S(2)}) collective-permute-start(bf16[1024,256]{1,0:T(8,128)(2,1)S(1)} %get-tuple-element.39), channel_id=1, source_target_pairs={{0,17},{1,16},{2,19},{3,18},{4,21},{5,20},{6,23},{7,22},{16,1},{17... | collective-permute-start | bytes 1572872 | tf_op jit(solution)/shard_map/ppermute | solution.py:176
  31.8 6.4 %collective-permute-done.1 = bf16[768,256]{1,0:T(8,128)(2,1)} collective-permute-done((bf16[768,256]{1,0:T(8,128)(2,1)S(1)}, bf16[768,256]{1,0:T(8,128)(2,1)}, u32[]{:S(2)}, u32[]{:S(2)}) %collective-permute-start.1) | collective-permute-done | bytes 393248 | tf_op jit(solution)/shard_map/ppermute | solution.py:176
  38.2 4.6 %copy-done = bf16[1,1,1,2,6,2048,256]{6,5,4,3,2,1,0:T(8,128)(2,1)S(1)} copy-done((bf16[1,1,1,2,6,2048,256]{6,5,4,3,2,1,0:T(8,128)(2,1)S(1)}, bf16[1,1,1,2,6,2048,256]{6,5,4,3,2,1,0:T(8,128)(2,1)}, u32[]{:S(2)}) %copy-start) | copy-done | bytes 12582936
  42.8 9.9 %shard_map.87 = f32[6,8,128]{2,1,0:T(8,128)S(1)} custom-call(s32[1,6]{1,0:T(1,128)S(1)} %copy-done.2, bf16[6,8,128]{2,1,0:T(8,128)(2,1)S(1)} %bitcast.45, bf16[2,6,2048,256]{3,2,1,0:T(8,128)(2,1)S(1)} %bitcast.43, bf16[2,6,2048,256]{3,2,1,0:T(8,128)(2,1)S(1)} %bitcast.44), custom_call_target="tpu_custom_call" | custom-call | flops 100663296 | bytes 12582912 | tf_op jit(solution)/shard_map/pallas_call | solution.py:211
  52.7 4.6 %fusion = f32[2,6,4096]{2,1,0:T(8,128)S(1)} fusion(bf16[1,1,1,1024,4096]{4,3,2,1,0:T(8,128)(2,1)} %param.10, bf16[1,6,1024]{2,1,0:T(8,128)(2,1)S(1)} %get-tuple-element.47, bf16[1,6,1024]{2,1,0:T(8,128)(2,1)S(1)} %get-tuple-element.46), kind=kOutput, calls=%fused_computation | convolution fusion | flops 100675584 | bytes 8609792 | tf_op jit(solution)/shard_map/jrs,sd->jrd/dot_general | solution.py:238
  57.4 2.7 %collective-permute-start.2 = (f32[2,6,2048]{2,1,0:T(8,128)S(1)}, f32[2,6,2048]{2,1,0:T(8,128)S(1)}, u32[]{:S(2)}, u32[]{:S(2)}) collective-permute-start(f32[2,6,2048]{2,1,0:T(8,128)S(1)} %constant_dynamic-slice_fusion.2), channel_id=1, source_target_pairs={{0,4},{1,5},{2,6},{3,7},{4,0},{5,1},{6,2},{7,3},{8,12},{9,13},{10,... | collective-permute-start | bytes 294920 | tf_op jit(solution)/shard_map/ppermute | solution.py:25
  60.1 1.8 %bitcast_dynamic-update-slice_fusion.7 = bf16[1,1,1,2,4096,256]{5,4,3,2,1,0:T(8,128)(2,1)} fusion(bf16[1,1,1,2,4096,256]{5,4,3,2,1,0:T(8,128)(2,1)} %bitcast_dynamic-update-slice_fusion.8, s32[]{:T(128)S(6)} %select_n.109, bf16[768,256]{1,0:T(8,128)(2,1)} %collective-permute-done), kind=kLoop, calls=%fused_computation.9 | loop fusion | bytes 786436 | tf_op jit(solution)/shard_map/dynamic_update_slice | solution.py:287
  61.9 1.8 %bitcast_dynamic-update-slice_fusion.6 = bf16[1,1,1,2,4096,256]{5,4,3,2,1,0:T(8,128)(2,1)} fusion(bf16[1,1,1,2,4096,256]{5,4,3,2,1,0:T(8,128)(2,1)} %bitcast_dynamic-update-slice_fusion.7, s32[]{:T(128)S(6)} %select_n.110, bf16[768,256]{1,0:T(8,128)(2,1)} %collective-permute-done.1), kind=kLoop, calls=%fused_computation.8 | loop fusion | bytes 786436 | tf_op jit(solution)/shard_map/dynamic_update_slice | solution.py:287
  63.6 1.1 %collective-permute-done.2 = f32[2,6,2048]{2,1,0:T(8,128)S(1)} collective-permute-done((f32[2,6,2048]{2,1,0:T(8,128)S(1)}, f32[2,6,2048]{2,1,0:T(8,128)S(1)}, u32[]{:S(2)}, u32[]{:S(2)}) %collective-permute-start.2) | collective-permute-done | bytes 98336 | tf_op jit(solution)/shard_map/ppermute | solution.py:25
  65.6 1.9 %bitcast_dynamic-update-slice_fusion.3 = bf16[1,1,1,2,4096,256]{5,4,3,2,1,0:T(8,128)(2,1)} fusion(bf16[1,1,1,2,4096,256]{5,4,3,2,1,0:T(8,128)(2,1)} %bitcast_dynamic-update-slice_fusion.6, s32[]{:T(128)S(6)} %select_n.109, bf16[1024,256]{1,0:T(8,128)(2,1)} %collective-permute-done.7), kind=kLoop, calls=%fused_computation.5 | loop fusion | bytes 1048580 | tf_op jit(solution)/shard_map/dynamic_update_slice | solution.py:287
  67.5 1.6 %collective-permute-done.3 = f32[2,6,1024]{2,1,0:T(8,128)S(1)} collective-permute-done((f32[2,6,1024]{2,1,0:T(8,128)S(1)}, f32[2,6,1024]{2,1,0:T(8,128)S(1)}, u32[]{:S(2)}, u32[]{:S(2)}) %collective-permute-start.3) | collective-permute-done | bytes 49184 | tf_op jit(solution)/shard_map/ppermute | solution.py:25
  69.2 1.6 %collective-permute-start.4 = (f32[2,6,512]{2,1,0:T(8,128)S(1)}, f32[2,6,512]{2,1,0:T(8,128)S(1)}, u32[]{:S(2)}, u32[]{:S(2)}) collective-permute-start(f32[2,6,512]{2,1,0:T(8,128)S(1)} %constant_dynamic-slice_fusion), channel_id=1, source_target_pairs={{0,1},{1,0},{2,3},{3,2},{4,5},{5,4},{6,7},{7,6},{8,9},{9,8},{10,11... | collective-permute-start | bytes 73736 | tf_op jit(solution)/shard_map/ppermute | solution.py:25
  70.8 1.9 %bitcast_dynamic-update-slice_fusion.2 = bf16[1,1,1,2,4096,256]{5,4,3,2,1,0:T(8,128)(2,1)} fusion(bf16[1,1,1,2,4096,256]{5,4,3,2,1,0:T(8,128)(2,1)} %bitcast_dynamic-update-slice_fusion.3, s32[]{:T(128)S(6)} %select_n.110, bf16[1024,256]{1,0:T(8,128)(2,1)} %collective-permute-done.8), kind=kLoop, calls=%fused_computation.4 | loop fusion | bytes 1048580 | tf_op jit(solution)/shard_map/dynamic_update_slice | solution.py:287
  72.7 8.1 %collective-permute-done.4 = f32[2,6,512]{2,1,0:T(8,128)S(1)} collective-permute-done((f32[2,6,512]{2,1,0:T(8,128)S(1)}, f32[2,6,512]{2,1,0:T(8,128)S(1)}, u32[]{:S(2)}, u32[]{:S(2)}) %collective-permute-start.4) | collective-permute-done | bytes 24608 | tf_op jit(solution)/shard_map/ppermute | solution.py:25
  80.7 1.4 %collective-permute-start.11 = (bf16[768,256]{1,0:T(8,128)(2,1)S(1)}, bf16[768,256]{1,0:T(8,128)(2,1)S(1)}, u32[]{:S(2)}, u32[]{:S(2)}) collective-permute-start(bf16[768,256]{1,0:T(8,128)(2,1)S(1)} %get-tuple-element.40), channel_id=1, source_target_pairs={{0,16},{1,17},{2,18},{3,19},{4,20},{5,21},{6,22},{7,23},{16,0},{17... | collective-permute-start | bytes 1179656 | tf_op jit(solution)/shard_map/ppermute | solution.py:176
  82.2 1.9 %bitcast_dynamic-update-slice_fusion.1 = bf16[1,1,1,2,4096,256]{5,4,3,2,1,0:T(8,128)(2,1)} fusion(bf16[1,1,1,2,4096,256]{5,4,3,2,1,0:T(8,128)(2,1)} %bitcast_dynamic-update-slice_fusion.2, s32[]{:T(128)S(6)} %select_n.109, bf16[1024,256]{1,0:T(8,128)(2,1)} %collective-permute-done.9), kind=kLoop, calls=%fused_computation.3 | loop fusion | bytes 1048580 | tf_op jit(solution)/shard_map/dynamic_update_slice | solution.py:287
  84.0 1.5 %collective-permute-start.12 = (bf16[768,256]{1,0:T(8,128)(2,1)S(1)}, bf16[768,256]{1,0:T(8,128)(2,1)S(1)}, u32[]{:S(2)}, u32[]{:S(2)}) collective-permute-start(bf16[768,256]{1,0:T(8,128)(2,1)S(1)} %get-tuple-element.41), channel_id=1, source_target_pairs={{0,17},{1,16},{2,19},{3,18},{4,21},{5,20},{6,23},{7,22},{16,1},{17... | collective-permute-start | bytes 1179656 | tf_op jit(solution)/shard_map/ppermute | solution.py:176
  85.5 1.9 %bitcast_dynamic-update-slice_fusion = bf16[1,1,1,2,4096,256]{5,4,3,2,1,0:T(8,128)(2,1)} fusion(bf16[1,1,1,2,4096,256]{5,4,3,2,1,0:T(8,128)(2,1)} %bitcast_dynamic-update-slice_fusion.1, s32[]{:T(128)S(6)} %select_n.110, bf16[1024,256]{1,0:T(8,128)(2,1)} %collective-permute-done.10), kind=kLoop, calls=%fused_computation.2 | loop fusion | bytes 1048580 | tf_op jit(solution)/shard_map/dynamic_update_slice | solution.py:287
  87.4 1.5 %collective-permute-start.13 = (bf16[128,256]{1,0:T(8,128)(2,1)S(1)}, bf16[128,256]{1,0:T(8,128)(2,1)S(1)}, u32[]{:S(2)}, u32[]{:S(2)}) collective-permute-start(bf16[128,256]{1,0:T(8,128)(2,1)S(1)} %get-tuple-element.42), channel_id=1, source_target_pairs={{0,16},{1,17},{2,18},{3,19},{4,20},{5,21},{6,22},{7,23},{16,0},{17... | collective-permute-start | bytes 196616 | tf_op jit(solution)/shard_map/ppermute | solution.py:176
  90.0 2.7 %collective-permute-done.11 = bf16[768,256]{1,0:T(8,128)(2,1)S(1)} collective-permute-done((bf16[768,256]{1,0:T(8,128)(2,1)S(1)}, bf16[768,256]{1,0:T(8,128)(2,1)S(1)}, u32[]{:S(2)}, u32[]{:S(2)}) %collective-permute-start.11) | collective-permute-done | bytes 393248 | tf_op jit(solution)/shard_map/ppermute | solution.py:176
  93.5 6.3 %collective-permute-done.12 = bf16[768,256]{1,0:T(8,128)(2,1)S(1)} collective-permute-done((bf16[768,256]{1,0:T(8,128)(2,1)S(1)}, bf16[768,256]{1,0:T(8,128)(2,1)S(1)}, u32[]{:S(2)}, u32[]{:S(2)}) %collective-permute-start.12) | collective-permute-done | bytes 393248 | tf_op jit(solution)/shard_map/ppermute | solution.py:176
  (37 shorter events, 5.2 us)
Async XLA Ops:
  0.6 7.8 %copy-start.1 = (s32[1,1,1,256]{3,2,1,0:T(1,128)S(1)}, s32[1,1,1,256]{3,2,1,0:T(1,128)}, u32[]{:S(2)}) copy-start(s32[1,1,1,256]{3,2,1,0:T(1,128)} %param.12) | copy-start | bytes 3076
  3.2 18.4 %collective-permute-start.5 = (bf16[384,256]{1,0:T(8,128)(2,1)}, bf16[384,256]{1,0:T(8,128)(2,1)}, u32[]{:S(2)}, u32[]{:S(2)}) collective-permute-start(bf16[384,256]{1,0:T(8,128)(2,1)} %get-tuple-element.32), channel_id=1, source_target_pairs={{0,16},{1,17},{2,18},{3,19},{4,20},{5,21},{6,22},{7,23},{16,0},{17... | collective-permute-start | bytes 589832 | tf_op jit(solution)/shard_map/ppermute | solution.py:176
  6.2 18.0 %collective-permute-start.6 = (bf16[384,256]{1,0:T(8,128)(2,1)}, bf16[384,256]{1,0:T(8,128)(2,1)}, u32[]{:S(2)}, u32[]{:S(2)}) collective-permute-start(bf16[384,256]{1,0:T(8,128)(2,1)} %get-tuple-element.33), channel_id=1, source_target_pairs={{0,17},{1,16},{2,19},{3,18},{4,21},{5,20},{6,23},{7,22},{16,1},{17... | collective-permute-start | bytes 589832 | tf_op jit(solution)/shard_map/ppermute | solution.py:176
  8.4 29.8 %copy-start.3 = (bf16[1,1,1,6,1024]{4,3,2,1,0:T(8,128)(2,1)S(1)}, bf16[1,1,1,6,1024]{4,3,2,1,0:T(8,128)(2,1)}, u32[]{:S(2)}) copy-start(bf16[1,1,1,6,1024]{4,3,2,1,0:T(8,128)(2,1)} %param.7) | copy-start | bytes 36868
  8.4 29.8 %copy-start.2 = (s32[1,6]{1,0:T(1,128)S(1)}, s32[1,6]{1,0:T(1,128)}, u32[]{:S(2)}) copy-start(s32[1,6]{1,0:T(1,128)} %lengths_ref.1) | copy-start | bytes 76
  17.4 12.4 %collective-permute-start = (bf16[768,256]{1,0:T(8,128)(2,1)}, bf16[768,256]{1,0:T(8,128)(2,1)}, u32[]{:S(2)}, u32[]{:S(2)}) collective-permute-start(bf16[768,256]{1,0:T(8,128)(2,1)} %get-tuple-element.23), channel_id=1, source_target_pairs={{0,16},{1,17},{2,18},{3,19},{4,20},{5,21},{6,22},{7,23},{16,0},{17... | collective-permute-start | bytes 1179656 | tf_op jit(solution)/shard_map/ppermute | solution.py:176
  19.5 18.7 %collective-permute-start.1 = (bf16[768,256]{1,0:T(8,128)(2,1)S(1)}, bf16[768,256]{1,0:T(8,128)(2,1)}, u32[]{:S(2)}, u32[]{:S(2)}) collective-permute-start(bf16[768,256]{1,0:T(8,128)(2,1)S(1)} %get-tuple-element.24), channel_id=1, source_target_pairs={{0,17},{1,16},{2,19},{3,18},{4,21},{5,20},{6,23},{7,22},{16,1},{17... | collective-permute-start | bytes 1179656 | tf_op jit(solution)/shard_map/ppermute | solution.py:176
  19.5 46.1 %collective-permute-start.7 = (bf16[1024,256]{1,0:T(8,128)(2,1)S(1)}, bf16[1024,256]{1,0:T(8,128)(2,1)}, u32[]{:S(2)}, u32[]{:S(2)}) collective-permute-start(bf16[1024,256]{1,0:T(8,128)(2,1)S(1)} %get-tuple-element.36), channel_id=1, source_target_pairs={{0,16},{1,17},{2,18},{3,19},{4,20},{5,21},{6,22},{7,23},{16,0},{17... | collective-permute-start | bytes 1572872 | tf_op jit(solution)/shard_map/ppermute | solution.py:176
  21.6 49.2 %collective-permute-start.8 = (bf16[1024,256]{1,0:T(8,128)(2,1)S(1)}, bf16[1024,256]{1,0:T(8,128)(2,1)}, u32[]{:S(2)}, u32[]{:S(2)}) collective-permute-start(bf16[1024,256]{1,0:T(8,128)(2,1)S(1)} %get-tuple-element.37), channel_id=1, source_target_pairs={{0,17},{1,16},{2,19},{3,18},{4,21},{5,20},{6,23},{7,22},{16,1},{17... | collective-permute-start | bytes 1572872 | tf_op jit(solution)/shard_map/ppermute | solution.py:176
  24.2 57.9 %collective-permute-start.9 = (bf16[1024,256]{1,0:T(8,128)(2,1)S(1)}, bf16[1024,256]{1,0:T(8,128)(2,1)}, u32[]{:S(2)}, u32[]{:S(2)}) collective-permute-start(bf16[1024,256]{1,0:T(8,128)(2,1)S(1)} %get-tuple-element.38), channel_id=1, source_target_pairs={{0,16},{1,17},{2,18},{3,19},{4,20},{5,21},{6,22},{7,23},{16,0},{17... | collective-permute-start | bytes 1572872 | tf_op jit(solution)/shard_map/ppermute | solution.py:176
  29.8 55.7 %collective-permute-start.10 = (bf16[1024,256]{1,0:T(8,128)(2,1)S(1)}, bf16[1024,256]{1,0:T(8,128)(2,1)}, u32[]{:S(2)}, u32[]{:S(2)}) collective-permute-start(bf16[1024,256]{1,0:T(8,128)(2,1)S(1)} %get-tuple-element.39), channel_id=1, source_target_pairs={{0,17},{1,16},{2,19},{3,18},{4,21},{5,20},{6,23},{7,22},{16,1},{17... | collective-permute-start | bytes 1572872 | tf_op jit(solution)/shard_map/ppermute | solution.py:176
  38.2 4.6 %copy-start = (bf16[1,1,1,2,6,2048,256]{6,5,4,3,2,1,0:T(8,128)(2,1)S(1)}, bf16[1,1,1,2,6,2048,256]{6,5,4,3,2,1,0:T(8,128)(2,1)}, u32[]{:S(2)}) copy-start(bf16[1,1,1,2,6,2048,256]{6,5,4,3,2,1,0:T(8,128)(2,1)} %param.8) | copy-start | bytes 37748740
  57.4 7.3 %collective-permute-start.2 = (f32[2,6,2048]{2,1,0:T(8,128)S(1)}, f32[2,6,2048]{2,1,0:T(8,128)S(1)}, u32[]{:S(2)}, u32[]{:S(2)}) collective-permute-start(f32[2,6,2048]{2,1,0:T(8,128)S(1)} %constant_dynamic-slice_fusion.2), channel_id=1, source_target_pairs={{0,4},{1,5},{2,6},{3,7},{4,0},{5,1},{6,2},{7,3},{8,12},{9,13},{10,... | collective-permute-start | bytes 294920 | tf_op jit(solution)/shard_map/ppermute | solution.py:25
  64.8 4.3 %collective-permute-start.3 = (f32[2,6,1024]{2,1,0:T(8,128)S(1)}, f32[2,6,1024]{2,1,0:T(8,128)S(1)}, u32[]{:S(2)}, u32[]{:S(2)}) collective-permute-start(f32[2,6,1024]{2,1,0:T(8,128)S(1)} %constant_dynamic-slice_fusion.1), channel_id=1, source_target_pairs={{0,2},{1,3},{2,0},{3,1},{4,6},{5,7},{6,4},{7,5},{8,10},{9,11},{10,... | collective-permute-start | bytes 147464 | tf_op jit(solution)/shard_map/ppermute | solution.py:25
  69.2 11.6 %collective-permute-start.4 = (f32[2,6,512]{2,1,0:T(8,128)S(1)}, f32[2,6,512]{2,1,0:T(8,128)S(1)}, u32[]{:S(2)}, u32[]{:S(2)}) collective-permute-start(f32[2,6,512]{2,1,0:T(8,128)S(1)} %constant_dynamic-slice_fusion), channel_id=1, source_target_pairs={{0,1},{1,0},{2,3},{3,2},{4,5},{5,4},{6,7},{7,6},{8,9},{9,8},{10,11... | collective-permute-start | bytes 73736 | tf_op jit(solution)/shard_map/ppermute | solution.py:25
  80.7 12.1 %collective-permute-start.11 = (bf16[768,256]{1,0:T(8,128)(2,1)S(1)}, bf16[768,256]{1,0:T(8,128)(2,1)S(1)}, u32[]{:S(2)}, u32[]{:S(2)}) collective-permute-start(bf16[768,256]{1,0:T(8,128)(2,1)S(1)} %get-tuple-element.40), channel_id=1, source_target_pairs={{0,16},{1,17},{2,18},{3,19},{4,20},{5,21},{6,22},{7,23},{16,0},{17... | collective-permute-start | bytes 1179656 | tf_op jit(solution)/shard_map/ppermute | solution.py:176
  84.0 15.8 %collective-permute-start.12 = (bf16[768,256]{1,0:T(8,128)(2,1)S(1)}, bf16[768,256]{1,0:T(8,128)(2,1)S(1)}, u32[]{:S(2)}, u32[]{:S(2)}) collective-permute-start(bf16[768,256]{1,0:T(8,128)(2,1)S(1)} %get-tuple-element.41), channel_id=1, source_target_pairs={{0,17},{1,16},{2,19},{3,18},{4,21},{5,20},{6,23},{7,22},{16,1},{17... | collective-permute-start | bytes 1179656 | tf_op jit(solution)/shard_map/ppermute | solution.py:176
  87.4 13.2 %collective-permute-start.13 = (bf16[128,256]{1,0:T(8,128)(2,1)S(1)}, bf16[128,256]{1,0:T(8,128)(2,1)S(1)}, u32[]{:S(2)}, u32[]{:S(2)}) collective-permute-start(bf16[128,256]{1,0:T(8,128)(2,1)S(1)} %get-tuple-element.42), channel_id=1, source_target_pairs={{0,16},{1,17},{2,18},{3,19},{4,20},{5,21},{6,22},{7,23},{16,0},{17... | collective-permute-start | bytes 196616 | tf_op jit(solution)/shard_map/ppermute | solution.py:176
  88.9 12.3 %collective-permute-start.14 = (bf16[128,256]{1,0:T(8,128)(2,1)S(1)}, bf16[128,256]{1,0:T(8,128)(2,1)S(1)}, u32[]{:S(2)}, u32[]{:S(2)}) collective-permute-start(bf16[128,256]{1,0:T(8,128)(2,1)S(1)} %get-tuple-element.43), channel_id=1, source_target_pairs={{0,17},{1,16},{2,19},{3,18},{4,21},{5,20},{6,23},{7,22},{16,1},{17... | collective-permute-start | bytes 196616 | tf_op jit(solution)/shard_map/ppermute | solution.py:176

commit v3 on v2

--- a/solution.py
+++ b/solution.py
@@ -9,7 +9,7 @@
 
 HEADS = 32
 KV_HEADS = 8
-SHARES = (3, 6, 8, 8, 6, 1)
+SHARES = (3, 6, 8, 9, 5, 1)
 
 
 def halved_sum(value, axis):
@@ -38,17 +38,18 @@
     chunk_refs, (held, edge, blank, edge_sem, sem) = rest[:-5], rest[-5:]
     block_len = edge.shape[1]
     units = sent_units(paired)
-    fetches = []
-    for way in range(2):
-        fetches.append(
-            pltpu.make_async_copy(stored_ref.at[units[way]], held.at[way], edge_sem.at[way])
-        )
-        fetches[way].start()
+    pieces = 8
+    span = held.shape[1] // pieces
+    for piece in range(pieces):
+        for way in range(2):
+            here = pl.ds(piece * span, span)
+            pltpu.make_async_copy(
+                stored_ref.at[units[way], here], held.at[way, here], edge_sem
+            ).start()
     length = length_ref[0]
     full = length // block_len
     blank[...] = jnp.zeros_like(blank)
-    for fetch in fetches:
-        fetch.wait()
+    pltpu.make_async_copy(held, held, edge_sem).wait()
 
     for part, start in enumerate(starts):
         count = chunk_refs[2 * part].shape[0] // block_len
@@ -94,23 +95,23 @@
         pltpu.make_async_copy(chunk_ref, chunk_ref, sem).wait()
 
 
-def first_kernel(paired, order_ref, stored_ref, same_ref, other_ref, sem):
+def first_kernel(start, paired, order_ref, stored_ref, same_ref, other_ref, sem):
     block_len = stored_ref.shape[2]
     units = sent_units(paired)
     for i in range(same_ref.shape[0] // block_len):
         for unit, chunk_ref in zip(units, (same_ref, other_ref)):
             pltpu.make_async_copy(
-                stored_ref.at[unit, order_ref[i]], chunk_ref.at[pl.ds(i * block_len, block_len)], sem
+                stored_ref.at[unit, order_ref[start + i]], chunk_ref.at[pl.ds(i * block_len, block_len)], sem
             ).start()
     for chunk_ref in (same_ref, other_ref):
         pltpu.make_async_copy(chunk_ref, chunk_ref, sem).wait()
 
 
-def first_chunks(stored, block_ids, paired, count):
+def first_chunks(stored, block_ids, paired, start, count):
     block_len, lane_width = stored.shape[2:]
     chunk_shape = jax.ShapeDtypeStruct((count * block_len, lane_width), stored.dtype)
     return pl.pallas_call(
-        functools.partial(first_kernel, paired),
+        functools.partial(first_kernel, start, paired),
         out_shape=[chunk_shape] * 2,
         in_specs=[
             pl.BlockSpec(memory_space=pltpu.SMEM),
@@ -153,12 +154,47 @@
             pltpu.VMEM((2,) + stored.shape[1:], stored.dtype),
             pltpu.VMEM((2, block_len, lane_width), stored.dtype),
             pltpu.VMEM((block_len, lane_width), stored.dtype),
-            pltpu.SemaphoreType.DMA((2,)),
+            pltpu.SemaphoreType.DMA,
             pltpu.SemaphoreType.DMA,
         ],
         compiler_params=pltpu.CompilerParams(vmem_limit_bytes=48 * 1024 * 1024),
         cost_estimate=pl.CostEstimate(flops=0, bytes_accessed=4 * total, transcendentals=0),
     )(block_ids, sent_length, stored)
+
+
+def place_kernel(starts, slot_of, arrived_ref, *rest):
+    landed_refs, (out_ref, sems) = rest[:-2], rest[-2:]
+    slots = slot_of()
+    copies = []
+    for at, (landed_ref, (start, way)) in enumerate(zip(landed_refs, starts)):
+        copies.append(
+            pltpu.make_async_copy(
+                landed_ref, out_ref.at[slots[way], pl.ds(start, landed_ref.shape[0])], sems.at[at]
+            )
+        )
+    for copy in copies:
+        copy.start()
+    for copy in copies:
+        copy.wait()
+
+
+def place_last(arrived, pieces, starts, paired):
+    return pl.pallas_call(
+        functools.partial(place_kernel, starts, functools.partial(landing_slots, paired)),
+        out_shape=jax.ShapeDtypeStruct(arrived.shape, arrived.dtype),
+        in_specs=[pl.BlockSpec(memory_space=pltpu.HBM)] + [pl.BlockSpec(memory_space=pl.ANY)] * len(pieces),
+        out_specs=pl.BlockSpec(memory_space=pltpu.HBM),
+        scratch_shapes=[pltpu.SemaphoreType.DMA((len(pieces),))],
+        input_output_aliases={0: 0},
+    )(arrived, *pieces)
+
+
+def landing_slots(paired):
+    parity = lax.axis_index("tensor") % 2
+    if paired:
+        return parity, 1 - parity
+    second = lax.axis_index("inst")
+    return second * parity, 1 - second * parity
 
 
 def cuts(block_count):
@@ -256,13 +292,8 @@
     unit_count, block_count, block_len, lane_width = stored.shape
     block_ids = block_order[0, 0, 0]
     starts, counts = cuts(block_count)
-    chunks = list(first_chunks(stored, block_ids, paired, counts[0]))
+    chunks = list(first_chunks(stored, block_ids, paired, starts[0], counts[0]))
     chunks += ordered_chunks(stored, block_ids, sent_length, paired, starts[1:], counts[1:])
-    if paired:
-        same_slot, other_slot = parity, 1 - parity
-    else:
-        same_slot = jnp.where(second, parity, 0)
-        other_slot = jnp.where(second, 1 - parity, 1)
     arrived = room((unit_count, block_count * block_len, lane_width), stored.dtype)
     landed = [None] * len(chunks)
 
@@ -281,10 +312,17 @@
     totals = halved_sum(partial_value, "tensor")
     totals, *chunks[2 * early :] = lax.optimization_barrier((totals, *chunks[2 * early :]))
     send(range(early, len(counts)))
+    slots = landing_slots(paired)
+    last = []
     for part, start in enumerate(starts):
-        for way, slot in enumerate((same_slot, other_slot)):
-            place = (slot, start * block_len, 0)
-            arrived = lax.dynamic_update_slice(arrived, landed[2 * part + way][None], place)
+        for way in range(2):
+            piece = landed[2 * part + way]
+            if 2 * part + way >= len(landed) - 3:
+                last.append((piece, (start * block_len, way)))
+            else:
+                place = (slots[way], start * block_len, 0)
+                arrived = lax.dynamic_update_slice(arrived, piece[None], place)
+    arrived = place_last(arrived, [piece for piece, _ in last], [at for _, at in last], paired)
     return (totals[None], arrived[None, None, None])
 
 

time: 103 us -> 119 us (1.16)
  Pallas kernels: 21.5 us -> 37 us
    pallas_call x1 -> x2, Pallas kernels: 2.58 us -> 17.6 us  [the longest x1 15 us: place_last(): pl.pallas_call(functools.partial(place_kernel, starts, functools.partial(...]
    unnamed x10 -> x20, local copies, waits for them, and re-layouts: 5.22 us -> 7.28 us
    ppermute x3, waiting for transfers between devices: 10.8 us -> 12.8 us  [halved_sum(): lax.ppermute(given, axis, [(i, i ^ step) for i in range(size)])]
    dynamic_update_slice x12 -> x9, local copies, waits for them, and re-layouts: 17 us -> 15.1 us  [per_device(): arrived = lax.dynamic_update_slice(arrived, piece[None], place)]
    ppermute x12, waiting for transfers between devices: 17.4 us -> 16.2 us  [crossed(): return lax.ppermute(chunk, ('inst', 'tensor'), route)]
  transfers between devices with their start and end apart: 15 -> 15, of which waited for: 7 -> 8; matrix products, arithmetic and copies ran while one was open for 22% -> 17% of each run, Pallas kernels for 19% -> 16%
where the time goes in v3:
time: 119 us; the launch traced here: 118 us
  Pallas kernels  37 us (31%)
  waiting for transfers between devices  29 us (24%)
  starting transfers between devices  23.7 us (20%)
  local copies, waits for them, and re-layouts  22.6 us (19%)
  matrix products  4.64 us (4%)
  between operations  1.46 us (1%)
    ppermute x12, starting transfers between devices, crossed(): return lax.ppermute(chunk, ('inst', 'tensor'), route)  18.1 us
    ppermute x12, waiting for transfers between devices, crossed(): return lax.ppermute(chunk, ('inst', 'tensor'), route)  16.2 us
    dynamic_update_slice x9, local copies, waits for them, and re-layouts, per_device(): arrived = lax.dynamic_update_slice(arrived, piece[None], place)  15.1 us
    pallas_call x1, Pallas kernels, place_last(): pl.pallas_call(functools.partial(place_kernel, starts, functools.partial(...  15 us
    ppermute x3, waiting for transfers between devices, halved_sum(): lax.ppermute(given, axis, [(i, i ^ step) for i in range(size)])  12.8 us
    pallas_call x1, Pallas kernels, attend_slots(): pl.pallas_call(functools.partial(attend_kernel, HEADS // KV_HEADS), grid=...  9.9 us
    pallas_call x1, Pallas kernels, ordered_chunks(): pl.pallas_call(functools.partial(order_kernel, starts, paired), out_shape...  9.47 us
    unnamed x20, local copies, waits for them, and re-layouts  7.28 us
  transfers between devices with their start and end apart: 15, of which 8 were waited for; matrix products, arithmetic and copies ran while one was open for 17% of the time, Pallas kernels for 16%

profile of v3, /device:TPU:0, one launch (start us, length us, event | category | flops | bytes accessed | tf_op | source)
XLA Modules:
  0.0 118.4 jit_solution(13166897176656915661)
XLA Ops:
  0.6 2.6 %shard_map.89 = (bf16[384,256]{1,0:T(8,128)(2,1)}, bf16[384,256]{1,0:T(8,128)(2,1)}) custom-call(s32[256]{0:T(256)} %bitcast.40, bf16[2,256,16,256]{3,2,1,0:T(8,128)(2,1)} %bitcast.42), custom_call_target="tpu_custom_call" | custom-call | tf_op jit(solution)/shard_map/pallas_call | solution.py:113
  3.2 3.0 %collective-permute-start.5 = (bf16[384,256]{1,0:T(8,128)(2,1)}, bf16[384,256]{1,0:T(8,128)(2,1)}, u32[]{:S(2)}, u32[]{:S(2)}) collective-permute-start(bf16[384,256]{1,0:T(8,128)(2,1)} %get-tuple-element.32), channel_id=1, source_target_pairs={{0,16},{1,17},{2,18},{3,19},{4,20},{5,21},{6,22},{7,23},{16,0},{17... | collective-permute-start | bytes 589832 | tf_op jit(solution)/shard_map/ppermute | solution.py:212
  6.2 1.5 %collective-permute-start.6 = (bf16[384,256]{1,0:T(8,128)(2,1)}, bf16[384,256]{1,0:T(8,128)(2,1)}, u32[]{:S(2)}, u32[]{:S(2)}) collective-permute-start(bf16[384,256]{1,0:T(8,128)(2,1)} %get-tuple-element.33), channel_id=1, source_target_pairs={{0,17},{1,16},{2,19},{3,18},{4,21},{5,20},{6,23},{7,22},{16,1},{17... | collective-permute-start | bytes 589832 | tf_op jit(solution)/shard_map/ppermute | solution.py:212
  8.4 9.5 %shard_map.86 = (bf16[768,256]{1,0:T(8,128)(2,1)S(1)}, bf16[768,256]{1,0:T(8,128)(2,1)S(1)}, bf16[1024,256]{1,0:T(8,128)(2,1)S(1)}, bf16[1024,256]{1,0:T(8,128)(...) custom-call(s32[256]{0:T(256)S(1)} %bitcast.41, ...), custom_call_target="tpu_custom_call" | custom-call | bytes 7602176 | tf_op jit(solution)/shard_map/pallas_call | solution.py:144
  18.6 1.8 %collective-permute-start = (bf16[768,256]{1,0:T(8,128)(2,1)S(1)}, bf16[768,256]{1,0:T(8,128)(2,1)}, u32[]{:S(2)}, u32[]{:S(2)}) collective-permute-start(bf16[768,256]{1,0:T(8,128)(2,1)S(1)} %get-tuple-element.23), channel_id=1, source_target_pairs={{0,16},{1,17},{2,18},{3,19},{4,20},{5,21},{6,22},{7,23},{16,0},{17... | collective-permute-start | bytes 1179656 | tf_op jit(solution)/shard_map/ppermute | solution.py:212
  20.5 2.0 %collective-permute-start.7 = (bf16[1024,256]{1,0:T(8,128)(2,1)S(1)}, bf16[1024,256]{1,0:T(8,128)(2,1)}, u32[]{:S(2)}, u32[]{:S(2)}) collective-permute-start(bf16[1024,256]{1,0:T(8,128)(2,1)S(1)} %get-tuple-element.36), channel_id=1, source_target_pairs={{0,16},{1,17},{2,18},{3,19},{4,20},{5,21},{6,22},{7,23},{16,0},{17... | collective-permute-start | bytes 1572872 | tf_op jit(solution)/shard_map/ppermute | solution.py:212
  22.6 1.1 collective-permute-start.8
  23.7 1.6 %bitcast_dynamic-update-slice_fusion.8 = bf16[2,4096,256]{2,1,0:T(8,128)(2,1)} fusion(bf16[2,4096,256]{2,1,0:T(8,128)(2,1)} %shard_map.88, s32[]{:T(128)S(6)} %select_n.108, bf16[384,256]{1,0:T(8,128)(2,1)} %collective-permute-done.5), kind=kLoop, calls=%fused_computation.10 | loop fusion | bytes 393220 | tf_op jit(solution)/shard_map/dynamic_update_slice | solution.py:324
  25.4 1.8 %collective-permute-start.9 = (bf16[1152,256]{1,0:T(8,128)(2,1)S(1)}, bf16[1152,256]{1,0:T(8,128)(2,1)}, u32[]{:S(2)}, u32[]{:S(2)}) collective-permute-start(bf16[1152,256]{1,0:T(8,128)(2,1)S(1)} %get-tuple-element.38), channel_id=1, source_target_pairs={{0,16},{1,17},{2,18},{3,19},{4,20},{5,21},{6,22},{7,23},{16,0},{17... | collective-permute-start | bytes 1769480 | tf_op jit(solution)/shard_map/ppermute | solution.py:212
  27.2 1.6 %bitcast_dynamic-update-slice_fusion.7 = bf16[2,4096,256]{2,1,0:T(8,128)(2,1)} fusion(bf16[2,4096,256]{2,1,0:T(8,128)(2,1)} %bitcast_dynamic-update-slice_fusion.8, s32[]{:T(128)S(6)} %select_n.109, bf16[384,256]{1,0:T(8,128)(2,1)} %collective-permute-done.6), kind=kLoop, calls=%fused_computation.9 | loop fusion | bytes 393220 | tf_op jit(solution)/shard_map/dynamic_update_slice | solution.py:324
  28.8 2.0 %collective-permute-done = bf16[768,256]{1,0:T(8,128)(2,1)} collective-permute-done((bf16[768,256]{1,0:T(8,128)(2,1)S(1)}, bf16[768,256]{1,0:T(8,128)(2,1)}, u32[]{:S(2)}, u32[]{:S(2)}) %collective-permute-start) | collective-permute-done | bytes 393248 | tf_op jit(solution)/shard_map/ppermute | solution.py:212
  30.8 1.8 %collective-permute-start.10 = (bf16[1152,256]{1,0:T(8,128)(2,1)S(1)}, bf16[1152,256]{1,0:T(8,128)(2,1)}, u32[]{:S(2)}, u32[]{:S(2)}) collective-permute-start(bf16[1152,256]{1,0:T(8,128)(2,1)S(1)} %get-tuple-element.39), channel_id=1, source_target_pairs={{0,17},{1,16},{2,19},{3,18},{4,21},{5,20},{6,23},{7,22},{16,1},{17... | collective-permute-start | bytes 1769480 | tf_op jit(solution)/shard_map/ppermute | solution.py:212
  32.6 6.4 %collective-permute-done.1 = bf16[768,256]{1,0:T(8,128)(2,1)} collective-permute-done((bf16[768,256]{1,0:T(8,128)(2,1)S(1)}, bf16[768,256]{1,0:T(8,128)(2,1)}, u32[]{:S(2)}, u32[]{:S(2)}) %collective-permute-start.1) | collective-permute-done | bytes 393248 | tf_op jit(solution)/shard_map/ppermute | solution.py:212
  39.0 4.6 %copy-done = bf16[1,1,1,2,6,2048,256]{6,5,4,3,2,1,0:T(8,128)(2,1)S(1)} copy-done((bf16[1,1,1,2,6,2048,256]{6,5,4,3,2,1,0:T(8,128)(2,1)S(1)}, bf16[1,1,1,2,6,2048,256]{6,5,4,3,2,1,0:T(8,128)(2,1)}, u32[]{:S(2)}) %copy-start) | copy-done | bytes 12582936
  43.5 9.9 %shard_map.87 = f32[6,8,128]{2,1,0:T(8,128)S(1)} custom-call(s32[1,6]{1,0:T(1,128)S(1)} %copy-done.2, bf16[6,8,128]{2,1,0:T(8,128)(2,1)S(1)} %bitcast.39, bf16[2,6,2048,256]{3,2,1,0:T(8,128)(2,1)S(1)} %bitcast.37, bf16[2,6,2048,256]{3,2,1,0:T(8,128)(2,1)S(1)} %bitcast.38), custom_call_target="tpu_custom_call" | custom-call | flops 100663296 | bytes 12582912 | tf_op jit(solution)/shard_map/pallas_call | solution.py:247
  53.5 4.6 %fusion = f32[2,6,4096]{2,1,0:T(8,128)S(1)} fusion(bf16[1,1,1,1024,4096]{4,3,2,1,0:T(8,128)(2,1)} %param.10, bf16[1,6,1024]{2,1,0:T(8,128)(2,1)S(1)} %get-tuple-element.47, bf16[1,6,1024]{2,1,0:T(8,128)(2,1)S(1)} %get-tuple-element.46), kind=kOutput, calls=%fused_computation | convolution fusion | flops 100675584 | bytes 8609792 | tf_op jit(solution)/shard_map/jrs,sd->jrd/dot_general | solution.py:274
  58.2 2.9 %collective-permute-start.2 = (f32[2,6,2048]{2,1,0:T(8,128)S(1)}, f32[2,6,2048]{2,1,0:T(8,128)S(1)}, u32[]{:S(2)}, u32[]{:S(2)}) collective-permute-start(f32[2,6,2048]{2,1,0:T(8,128)S(1)} %constant_dynamic-slice_fusion.2), channel_id=1, source_target_pairs={{0,4},{1,5},{2,6},{3,7},{4,0},{5,1},{6,2},{7,3},{8,12},{9,13},{10,... | collective-permute-start | bytes 294920 | tf_op jit(solution)/shard_map/ppermute | solution.py:25
  61.1 1.8 %bitcast_dynamic-update-slice_fusion.5 = bf16[2,4096,256]{2,1,0:T(8,128)(2,1)} fusion(bf16[2,4096,256]{2,1,0:T(8,128)(2,1)} %bitcast_dynamic-update-slice_fusion.7, s32[]{:T(128)S(6)} %select_n.108, bf16[768,256]{1,0:T(8,128)(2,1)} %collective-permute-done), kind=kLoop, calls=%fused_computation.7 | loop fusion | bytes 786436 | tf_op jit(solution)/shard_map/dynamic_update_slice | solution.py:324
  62.8 1.8 %bitcast_dynamic-update-slice_fusion.4 = bf16[2,4096,256]{2,1,0:T(8,128)(2,1)} fusion(bf16[2,4096,256]{2,1,0:T(8,128)(2,1)} %bitcast_dynamic-update-slice_fusion.5, s32[]{:T(128)S(6)} %select_n.109, bf16[768,256]{1,0:T(8,128)(2,1)} %collective-permute-done.1), kind=kLoop, calls=%fused_computation.6 | loop fusion | bytes 786436 | tf_op jit(solution)/shard_map/dynamic_update_slice | solution.py:324
  66.5 1.9 %bitcast_dynamic-update-slice_fusion.3 = bf16[2,4096,256]{2,1,0:T(8,128)(2,1)} fusion(bf16[2,4096,256]{2,1,0:T(8,128)(2,1)} %bitcast_dynamic-update-slice_fusion.4, s32[]{:T(128)S(6)} %select_n.108, bf16[1024,256]{1,0:T(8,128)(2,1)} %collective-permute-done.7), kind=kLoop, calls=%fused_computation.5 | loop fusion | bytes 1048580 | tf_op jit(solution)/shard_map/dynamic_update_slice | solution.py:324
  68.4 1.5 %collective-permute-done.3 = f32[2,6,1024]{2,1,0:T(8,128)S(1)} collective-permute-done((f32[2,6,1024]{2,1,0:T(8,128)S(1)}, f32[2,6,1024]{2,1,0:T(8,128)S(1)}, u32[]{:S(2)}, u32[]{:S(2)}) %collective-permute-start.3) | collective-permute-done | bytes 49184 | tf_op jit(solution)/shard_map/ppermute | solution.py:25
  70.0 1.8 %collective-permute-start.4 = (f32[2,6,512]{2,1,0:T(8,128)S(1)}, f32[2,6,512]{2,1,0:T(8,128)S(1)}, u32[]{:S(2)}, u32[]{:S(2)}) collective-permute-start(f32[2,6,512]{2,1,0:T(8,128)S(1)} %constant_dynamic-slice_fusion), channel_id=1, source_target_pairs={{0,1},{1,0},{2,3},{3,2},{4,5},{5,4},{6,7},{7,6},{8,9},{9,8},{10,11... | collective-permute-start | bytes 73736 | tf_op jit(solution)/shard_map/ppermute | solution.py:25
  71.7 1.9 %bitcast_dynamic-update-slice_fusion.2 = bf16[2,4096,256]{2,1,0:T(8,128)(2,1)} fusion(bf16[2,4096,256]{2,1,0:T(8,128)(2,1)} %bitcast_dynamic-update-slice_fusion.3, s32[]{:T(128)S(6)} %select_n.109, bf16[1024,256]{1,0:T(8,128)(2,1)} %collective-permute-done.8), kind=kLoop, calls=%fused_computation.4 | loop fusion | bytes 1048580 | tf_op jit(solution)/shard_map/dynamic_update_slice | solution.py:324
  73.6 10.3 %collective-permute-done.4 = f32[2,6,512]{2,1,0:T(8,128)S(1)} collective-permute-done((f32[2,6,512]{2,1,0:T(8,128)S(1)}, f32[2,6,512]{2,1,0:T(8,128)S(1)}, u32[]{:S(2)}, u32[]{:S(2)}) %collective-permute-start.4) | collective-permute-done | bytes 24608 | tf_op jit(solution)/shard_map/ppermute | solution.py:25
  84.0 1.5 %collective-permute-start.11 = (bf16[640,256]{1,0:T(8,128)(2,1)S(1)}, bf16[640,256]{1,0:T(8,128)(2,1)S(1)}, u32[]{:S(2)}, u32[]{:S(2)}) collective-permute-start(bf16[640,256]{1,0:T(8,128)(2,1)S(1)} %copy-done.4), channel_id=1, source_target_pairs={{0,16},{1,17},{2,18},{3,19},{4,20},{5,21},{6,22},{7,23},{16,0},{17... | collective-permute-start | bytes 983048 | tf_op jit(solution)/shard_map/ppermute | solution.py:212
  85.5 1.3 %collective-permute-start.12 = (bf16[640,256]{1,0:T(8,128)(2,1)S(1)}, bf16[640,256]{1,0:T(8,128)(2,1)S(1)}, u32[]{:S(2)}, u32[]{:S(2)}) collective-permute-start(bf16[640,256]{1,0:T(8,128)(2,1)S(1)} %get-tuple-element.41), channel_id=1, source_target_pairs={{0,17},{1,16},{2,19},{3,18},{4,21},{5,20},{6,23},{7,22},{16,1},{17... | collective-permute-start | bytes 983048 | tf_op jit(solution)/shard_map/ppermute | solution.py:212
  86.8 1.7 %collective-permute-start.13 = (bf16[128,256]{1,0:T(8,128)(2,1)S(1)}, bf16[128,256]{1,0:T(8,128)(2,1)S(1)}, u32[]{:S(2)}, u32[]{:S(2)}) collective-permute-start(bf16[128,256]{1,0:T(8,128)(2,1)S(1)} %get-tuple-element.42), channel_id=1, source_target_pairs={{0,16},{1,17},{2,18},{3,19},{4,20},{5,21},{6,22},{7,23},{16,0},{17... | collective-permute-start | bytes 196616 | tf_op jit(solution)/shard_map/ppermute | solution.py:212
  89.6 1.9 %bitcast_dynamic-update-slice_fusion.1 = bf16[2,4096,256]{2,1,0:T(8,128)(2,1)} fusion(bf16[2,4096,256]{2,1,0:T(8,128)(2,1)} %bitcast_dynamic-update-slice_fusion.2, s32[]{:T(128)S(6)} %select_n.108, bf16[1152,256]{1,0:T(8,128)(2,1)} %collective-permute-done.9), kind=kLoop, calls=%fused_computation.3 | loop fusion | bytes 1179652 | tf_op jit(solution)/shard_map/dynamic_update_slice | solution.py:324
  91.5 1.9 %bitcast_dynamic-update-slice_fusion = bf16[2,4096,256]{2,1,0:T(8,128)(2,1)} fusion(bf16[2,4096,256]{2,1,0:T(8,128)(2,1)} %bitcast_dynamic-update-slice_fusion.1, s32[]{:T(128)S(6)} %select_n.109, bf16[1152,256]{1,0:T(8,128)(2,1)} %collective-permute-done.10), kind=kLoop, calls=%fused_computation.2 | loop fusion | bytes 1179652 | tf_op jit(solution)/shard_map/dynamic_update_slice | solution.py:324
  93.4 1.2 %collective-permute-done.11 = bf16[640,256]{1,0:T(8,128)(2,1)S(1)} collective-permute-done((bf16[640,256]{1,0:T(8,128)(2,1)S(1)}, bf16[640,256]{1,0:T(8,128)(2,1)S(1)}, u32[]{:S(2)}, u32[]{:S(2)}) %collective-permute-start.11) | collective-permute-done | bytes 327712 | tf_op jit(solution)/shard_map/ppermute | solution.py:212
  95.4 6.0 %collective-permute-done.13.rest_1_ = bf16[128,256]{1,0:T(8,128)(2,1)S(1)} collective-permute-done((bf16[128,256]{1,0:T(8,128)(2,1)S(1)}, bf16[128,256]{1,0:T(8,128)(2,1)S(1)}, u32[]{:S(2)}, u32[]{:S(2)}) %collective-permute-start.13) | collective-permute-done | bytes 65568 | tf_op jit(solution)/shard_map/ppermute | solution.py:212
  103.4 15.0 %shard_map.90 = bf16[2,4096,256]{2,1,0:T(8,128)(2,1)} custom-call(bf16[2,4096,256]{2,1,0:T(8,128)(2,1)} %bitcast_dynamic-update-slice_fusion.6.arrived_ref, bf16[640,256]{1,0:T(8,128)(2,1)} %copy-done.5, bf16[128,256]{1,0:T(8,128)(2,1)} %copy-done.6, bf16[128,256]{1,0:T(8,128)(2,1)} %copy-done.7), custom_call_target="tpu_custom_call", output_to_operand_aliasing={{}: (0, {})} | custom-call | tf_op jit(solution)/shard_map/pallas_call | solution.py:182
  (45 shorter events, 6.8 us)
Async XLA Ops:
  0.6 7.8 %copy-start.1 = (s32[1,1,1,256]{3,2,1,0:T(1,128)S(1)}, s32[1,1,1,256]{3,2,1,0:T(1,128)}, u32[]{:S(2)}) copy-start(s32[1,1,1,256]{3,2,1,0:T(1,128)} %param.12) | copy-start | bytes 3076
  3.2 19.3 %collective-permute-start.5 = (bf16[384,256]{1,0:T(8,128)(2,1)}, bf16[384,256]{1,0:T(8,128)(2,1)}, u32[]{:S(2)}, u32[]{:S(2)}) collective-permute-start(bf16[384,256]{1,0:T(8,128)(2,1)} %get-tuple-element.32), channel_id=1, source_target_pairs={{0,16},{1,17},{2,18},{3,19},{4,20},{5,21},{6,22},{7,23},{16,0},{17... | collective-permute-start | bytes 589832 | tf_op jit(solution)/shard_map/ppermute | solution.py:212
  6.2 19.1 %collective-permute-start.6 = (bf16[384,256]{1,0:T(8,128)(2,1)}, bf16[384,256]{1,0:T(8,128)(2,1)}, u32[]{:S(2)}, u32[]{:S(2)}) collective-permute-start(bf16[384,256]{1,0:T(8,128)(2,1)} %get-tuple-element.33), channel_id=1, source_target_pairs={{0,17},{1,16},{2,19},{3,18},{4,21},{5,20},{6,23},{7,22},{16,1},{17... | collective-permute-start | bytes 589832 | tf_op jit(solution)/shard_map/ppermute | solution.py:212
  8.4 30.6 %copy-start.8 = (bf16[1,1,1,6,1024]{4,3,2,1,0:T(8,128)(2,1)S(1)}, bf16[1,1,1,6,1024]{4,3,2,1,0:T(8,128)(2,1)}, u32[]{:S(2)}) copy-start(bf16[1,1,1,6,1024]{4,3,2,1,0:T(8,128)(2,1)} %param.7) | copy-start | bytes 36868
  8.4 30.6 %copy-start.2 = (s32[1,6]{1,0:T(1,128)S(1)}, s32[1,6]{1,0:T(1,128)}, u32[]{:S(2)}) copy-start(s32[1,6]{1,0:T(1,128)} %lengths_ref.1) | copy-start | bytes 76
  17.9 0.7 copy-start.3
  18.6 12.2 %collective-permute-start = (bf16[768,256]{1,0:T(8,128)(2,1)S(1)}, bf16[768,256]{1,0:T(8,128)(2,1)}, u32[]{:S(2)}, u32[]{:S(2)}) collective-permute-start(bf16[768,256]{1,0:T(8,128)(2,1)S(1)} %get-tuple-element.23), channel_id=1, source_target_pairs={{0,16},{1,17},{2,18},{3,19},{4,20},{5,21},{6,22},{7,23},{16,0},{17... | collective-permute-start | bytes 1179656 | tf_op jit(solution)/shard_map/ppermute | solution.py:212
  20.5 18.5 %collective-permute-start.1 = (bf16[768,256]{1,0:T(8,128)(2,1)S(1)}, bf16[768,256]{1,0:T(8,128)(2,1)}, u32[]{:S(2)}, u32[]{:S(2)}) collective-permute-start(bf16[768,256]{1,0:T(8,128)(2,1)S(1)} %get-tuple-element.24), channel_id=1, source_target_pairs={{0,17},{1,16},{2,19},{3,18},{4,21},{5,20},{6,23},{7,22},{16,1},{17... | collective-permute-start | bytes 1179656 | tf_op jit(solution)/shard_map/ppermute | solution.py:212
  20.5 46.1 %collective-permute-start.7 = (bf16[1024,256]{1,0:T(8,128)(2,1)S(1)}, bf16[1024,256]{1,0:T(8,128)(2,1)}, u32[]{:S(2)}, u32[]{:S(2)}) collective-permute-start(bf16[1024,256]{1,0:T(8,128)(2,1)S(1)} %get-tuple-element.36), channel_id=1, source_target_pairs={{0,16},{1,17},{2,18},{3,19},{4,20},{5,21},{6,22},{7,23},{16,0},{17... | collective-permute-start | bytes 1572872 | tf_op jit(solution)/shard_map/ppermute | solution.py:212
  22.6 49.2 %collective-permute-start.8 = (bf16[1024,256]{1,0:T(8,128)(2,1)S(1)}, bf16[1024,256]{1,0:T(8,128)(2,1)}, u32[]{:S(2)}, u32[]{:S(2)}) collective-permute-start(bf16[1024,256]{1,0:T(8,128)(2,1)S(1)} %get-tuple-element.37), channel_id=1, source_target_pairs={{0,17},{1,16},{2,19},{3,18},{4,21},{5,20},{6,23},{7,22},{16,1},{17... | collective-permute-start | bytes 1572872 | tf_op jit(solution)/shard_map/ppermute | solution.py:212
  25.4 63.7 %collective-permute-start.9 = (bf16[1152,256]{1,0:T(8,128)(2,1)S(1)}, bf16[1152,256]{1,0:T(8,128)(2,1)}, u32[]{:S(2)}, u32[]{:S(2)}) collective-permute-start(bf16[1152,256]{1,0:T(8,128)(2,1)S(1)} %get-tuple-element.38), channel_id=1, source_target_pairs={{0,16},{1,17},{2,18},{3,19},{4,20},{5,21},{6,22},{7,23},{16,0},{17... | collective-permute-start | bytes 1769480 | tf_op jit(solution)/shard_map/ppermute | solution.py:212
  30.8 60.7 %collective-permute-start.10 = (bf16[1152,256]{1,0:T(8,128)(2,1)S(1)}, bf16[1152,256]{1,0:T(8,128)(2,1)}, u32[]{:S(2)}, u32[]{:S(2)}) collective-permute-start(bf16[1152,256]{1,0:T(8,128)(2,1)S(1)} %get-tuple-element.39), channel_id=1, source_target_pairs={{0,17},{1,16},{2,19},{3,18},{4,21},{5,20},{6,23},{7,22},{16,1},{17... | collective-permute-start | bytes 1769480 | tf_op jit(solution)/shard_map/ppermute | solution.py:212
  39.0 4.6 %copy-start = (bf16[1,1,1,2,6,2048,256]{6,5,4,3,2,1,0:T(8,128)(2,1)S(1)}, bf16[1,1,1,2,6,2048,256]{6,5,4,3,2,1,0:T(8,128)(2,1)}, u32[]{:S(2)}) copy-start(bf16[1,1,1,2,6,2048,256]{6,5,4,3,2,1,0:T(8,128)(2,1)} %param.8) | copy-start | bytes 37748740
  58.2 25.8 %copy-start.4 = (bf16[640,256]{1,0:T(8,128)(2,1)S(1)}, bf16[640,256]{1,0:T(8,128)(2,1)}, u32[]{:S(2)}) copy-start(bf16[640,256]{1,0:T(8,128)(2,1)} %copy-done.3) | copy-start | bytes 983044
  58.2 7.3 %collective-permute-start.2 = (f32[2,6,2048]{2,1,0:T(8,128)S(1)}, f32[2,6,2048]{2,1,0:T(8,128)S(1)}, u32[]{:S(2)}, u32[]{:S(2)}) collective-permute-start(f32[2,6,2048]{2,1,0:T(8,128)S(1)} %constant_dynamic-slice_fusion.2), channel_id=1, source_target_pairs={{0,4},{1,5},{2,6},{3,7},{4,0},{5,1},{6,2},{7,3},{8,12},{9,13},{10,... | collective-permute-start | bytes 294920 | tf_op jit(solution)/shard_map/ppermute | solution.py:25
  65.6 4.3 %collective-permute-start.3 = (f32[2,6,1024]{2,1,0:T(8,128)S(1)}, f32[2,6,1024]{2,1,0:T(8,128)S(1)}, u32[]{:S(2)}, u32[]{:S(2)}) collective-permute-start(f32[2,6,1024]{2,1,0:T(8,128)S(1)} %constant_dynamic-slice_fusion.1), channel_id=1, source_target_pairs={{0,2},{1,3},{2,0},{3,1},{4,6},{5,7},{6,4},{7,5},{8,10},{9,11},{10,... | collective-permute-start | bytes 147464 | tf_op jit(solution)/shard_map/ppermute | solution.py:25
  70.0 14.0 %collective-permute-start.4 = (f32[2,6,512]{2,1,0:T(8,128)S(1)}, f32[2,6,512]{2,1,0:T(8,128)S(1)}, u32[]{:S(2)}, u32[]{:S(2)}) collective-permute-start(f32[2,6,512]{2,1,0:T(8,128)S(1)} %constant_dynamic-slice_fusion), channel_id=1, source_target_pairs={{0,1},{1,0},{2,3},{3,2},{4,5},{5,4},{6,7},{7,6},{8,9},{9,8},{10,11... | collective-permute-start | bytes 73736 | tf_op jit(solution)/shard_map/ppermute | solution.py:25
  84.0 10.7 %collective-permute-start.11 = (bf16[640,256]{1,0:T(8,128)(2,1)S(1)}, bf16[640,256]{1,0:T(8,128)(2,1)S(1)}, u32[]{:S(2)}, u32[]{:S(2)}) collective-permute-start(bf16[640,256]{1,0:T(8,128)(2,1)S(1)} %copy-done.4), channel_id=1, source_target_pairs={{0,16},{1,17},{2,18},{3,19},{4,20},{5,21},{6,22},{7,23},{16,0},{17... | collective-permute-start | bytes 983048 | tf_op jit(solution)/shard_map/ppermute | solution.py:212
  85.5 16.6 %collective-permute-start.12 = (bf16[640,256]{1,0:T(8,128)(2,1)S(1)}, bf16[640,256]{1,0:T(8,128)(2,1)S(1)}, u32[]{:S(2)}, u32[]{:S(2)}) collective-permute-start(bf16[640,256]{1,0:T(8,128)(2,1)S(1)} %get-tuple-element.41), channel_id=1, source_target_pairs={{0,17},{1,16},{2,19},{3,18},{4,21},{5,20},{6,23},{7,22},{16,1},{17... | collective-permute-start | bytes 983048 | tf_op jit(solution)/shard_map/ppermute | solution.py:212
  86.8 14.6 %collective-permute-start.13 = (bf16[128,256]{1,0:T(8,128)(2,1)S(1)}, bf16[128,256]{1,0:T(8,128)(2,1)S(1)}, u32[]{:S(2)}, u32[]{:S(2)}) collective-permute-start(bf16[128,256]{1,0:T(8,128)(2,1)S(1)} %get-tuple-element.42), channel_id=1, source_target_pairs={{0,16},{1,17},{2,18},{3,19},{4,20},{5,21},{6,22},{7,23},{16,0},{17... | collective-permute-start | bytes 196616 | tf_op jit(solution)/shard_map/ppermute | solution.py:212
  89.1 12.9 %collective-permute-start.14 = (bf16[128,256]{1,0:T(8,128)(2,1)S(1)}, bf16[128,256]{1,0:T(8,128)(2,1)S(1)}, u32[]{:S(2)}, u32[]{:S(2)}) collective-permute-start(bf16[128,256]{1,0:T(8,128)(2,1)S(1)} %get-tuple-element.43), channel_id=1, source_target_pairs={{0,17},{1,16},{2,19},{3,18},{4,21},{5,20},{6,23},{7,22},{16,1},{17... | collective-permute-start | bytes 196616 | tf_op jit(solution)/shard_map/ppermute | solution.py:212
  101.4 0.7 copy-start.6
  102.0 0.6 copy-start.7
  102.6 0.7 copy-start.5

commit v4 on v2

--- a/solution.py
+++ b/solution.py
@@ -9,7 +9,7 @@
 
 HEADS = 32
 KV_HEADS = 8
-SHARES = (3, 6, 8, 8, 6, 1)
+SHARES = (4, 5, 9, 8, 5, 1)
 
 
 def halved_sum(value, axis):

time: 103 us -> 101 us (0.981)
  waiting for transfers between devices: 28.2 us -> 25.5 us
  local copies, waits for them, and re-layouts: 22.5 us -> 24.5 us
  starting transfers between devices: 23.5 us -> 22.2 us
    ppermute x12, waiting for transfers between devices: 17.4 us -> 11.9 us  [crossed(): return lax.ppermute(chunk, ('inst', 'tensor'), route)]
    ppermute x3, waiting for transfers between devices: 10.8 us -> 13.6 us  [halved_sum(): lax.ppermute(given, axis, [(i, i ^ step) for i in range(size)])]
    unnamed x10 -> x16, local copies, waits for them, and re-layouts: 5.22 us -> 7.18 us
    ppermute x3, starting transfers between devices: 5.16 us -> 4.02 us  [halved_sum(): lax.ppermute(given, axis, [(i, i ^ step) for i in range(size)])]
  transfers between devices with their start and end apart: 15 -> 15, of which waited for: 7 -> 7; matrix products, arithmetic and copies ran while one was open for 22% -> 23% of each run, Pallas kernels for 19% -> 19%
where the time goes in v4:
time: 101 us
  waiting for transfers between devices  25.5 us (25%)
  local copies, waits for them, and re-layouts  24.5 us (24%)
  Pallas kernels  22.3 us (22%)
  starting transfers between devices  22.2 us (22%)
  matrix products  4.64 us (5%)
  between operations  1.44 us (1%)
    ppermute x12, starting transfers between devices, crossed(): return lax.ppermute(chunk, ('inst', 'tensor'), route)  18.1 us
    dynamic_update_slice x12, local copies, waits for them, and re-layouts, per_device(): lax.dynamic_update_slice(arrived, landed[2 * part + way][None], place)  17.1 us
    ppermute x3, waiting for transfers between devices, halved_sum(): lax.ppermute(given, axis, [(i, i ^ step) for i in range(size)])  13.6 us
    ppermute x12, waiting for transfers between devices, crossed(): return lax.ppermute(chunk, ('inst', 'tensor'), route)  11.9 us
    pallas_call x1, Pallas kernels, attend_slots(): pl.pallas_call(functools.partial(attend_kernel, HEADS // KV_HEADS), grid=...  9.9 us
    pallas_call x1, Pallas kernels, ordered_chunks(): pl.pallas_call(functools.partial(order_kernel, starts, paired), out_shape...  9.69 us
    unnamed x16, local copies, waits for them, and re-layouts  7.18 us
    dot_general x1, matrix products, project_layers(): jnp.einsum('jrs,sd->jrd', masked, weight, preferred_element_type=jnp.floa...  4.64 us
  transfers between devices with their start and end apart: 15, of which 7 were waited for; matrix products, arithmetic and copies ran while one was open for 23% of the time, Pallas kernels for 19%

profile of v4, /device:TPU:0, one launch (start us, length us, event | category | flops | bytes accessed | tf_op | source)
XLA Modules:
  0.0 100.6 jit_solution(5982611021923881598)
XLA Ops:
  0.6 2.7 %shard_map.89 = (bf16[512,256]{1,0:T(8,128)(2,1)}, bf16[512,256]{1,0:T(8,128)(2,1)}) custom-call(s32[256]{0:T(256)} %bitcast.46, bf16[2,256,16,256]{3,2,1,0:T(8,128)(2,1)} %bitcast.48), custom_call_target="tpu_custom_call" | custom-call | tf_op jit(solution)/shard_map/pallas_call | solution.py:112
  3.4 3.0 %collective-permute-start.5 = (bf16[512,256]{1,0:T(8,128)(2,1)}, bf16[512,256]{1,0:T(8,128)(2,1)}, u32[]{:S(2)}, u32[]{:S(2)}) collective-permute-start(bf16[512,256]{1,0:T(8,128)(2,1)} %get-tuple-element.32), channel_id=1, source_target_pairs={{0,16},{1,17},{2,18},{3,19},{4,20},{5,21},{6,22},{7,23},{16,0},{17... | collective-permute-start | bytes 786440 | tf_op jit(solution)/shard_map/ppermute | solution.py:176
  6.4 1.5 %collective-permute-start.6 = (bf16[512,256]{1,0:T(8,128)(2,1)}, bf16[512,256]{1,0:T(8,128)(2,1)}, u32[]{:S(2)}, u32[]{:S(2)}) collective-permute-start(bf16[512,256]{1,0:T(8,128)(2,1)} %get-tuple-element.33), channel_id=1, source_target_pairs={{0,17},{1,16},{2,19},{3,18},{4,21},{5,20},{6,23},{7,22},{16,1},{17... | collective-permute-start | bytes 786440 | tf_op jit(solution)/shard_map/ppermute | solution.py:176
  8.5 9.7 %shard_map.86 = (bf16[640,256]{1,0:T(8,128)(2,1)S(1)}, bf16[640,256]{1,0:T(8,128)(2,1)S(1)}, bf16[1152,256]{1,0:T(8,128)(2,1)S(1)}, bf16[1152,256]{1,0:T(8,128)(...) custom-call(s32[256]{0:T(256)S(1)} %bitcast.47, ...), custom_call_target="tpu_custom_call" | custom-call | bytes 7340032 | tf_op jit(solution)/shard_map/pallas_call | solution.py:143
  19.5 1.1 %collective-permute-start = (bf16[640,256]{1,0:T(8,128)(2,1)S(1)}, bf16[640,256]{1,0:T(8,128)(2,1)}, u32[]{:S(2)}, u32[]{:S(2)}) collective-permute-start(bf16[640,256]{1,0:T(8,128)(2,1)S(1)} %get-tuple-element.23), channel_id=1, source_target_pairs={{0,16},{1,17},{2,18},{3,19},{4,20},{5,21},{6,22},{7,23},{16,0},{17... | collective-permute-start | bytes 983048 | tf_op jit(solution)/shard_map/ppermute | solution.py:176
  21.0 1.6 %collective-permute-start.7 = (bf16[1152,256]{1,0:T(8,128)(2,1)S(1)}, bf16[1152,256]{1,0:T(8,128)(2,1)}, u32[]{:S(2)}, u32[]{:S(2)}) collective-permute-start(bf16[1152,256]{1,0:T(8,128)(2,1)S(1)} %get-tuple-element.36), channel_id=1, source_target_pairs={{0,16},{1,17},{2,18},{3,19},{4,20},{5,21},{6,22},{7,23},{16,0},{17... | collective-permute-start | bytes 1769480 | tf_op jit(solution)/shard_map/ppermute | solution.py:176
  22.7 1.9 %collective-permute-start.8 = (bf16[1152,256]{1,0:T(8,128)(2,1)S(1)}, bf16[1152,256]{1,0:T(8,128)(2,1)}, u32[]{:S(2)}, u32[]{:S(2)}) collective-permute-start(bf16[1152,256]{1,0:T(8,128)(2,1)S(1)} %get-tuple-element.37), channel_id=1, source_target_pairs={{0,17},{1,16},{2,19},{3,18},{4,21},{5,20},{6,23},{7,22},{16,1},{17... | collective-permute-start | bytes 1769480 | tf_op jit(solution)/shard_map/ppermute | solution.py:176
  24.6 1.7 %bitcast_dynamic-update-slice_fusion.9 = bf16[1,1,1,2,4096,256]{5,4,3,2,1,0:T(8,128)(2,1)} fusion(bf16[1,1,1,2,4096,256]{5,4,3,2,1,0:T(8,128)(2,1)} %bitcast.50, s32[]{:T(128)S(6)} %select_n.109, bf16[512,256]{1,0:T(8,128)(2,1)} %collective-permute-done.5), kind=kLoop, calls=%fused_computation.11 | loop fusion | bytes 524292 | tf_op jit(solution)/shard_map/dynamic_update_slice | solution.py:287
  26.3 3.9 %collective-permute-done = bf16[640,256]{1,0:T(8,128)(2,1)} collective-permute-done((bf16[640,256]{1,0:T(8,128)(2,1)S(1)}, bf16[640,256]{1,0:T(8,128)(2,1)}, u32[]{:S(2)}, u32[]{:S(2)}) %collective-permute-start) | collective-permute-done | bytes 327712 | tf_op jit(solution)/shard_map/ppermute | solution.py:176
  30.2 1.1 %collective-permute-start.9 = (bf16[1024,256]{1,0:T(8,128)(2,1)S(1)}, bf16[1024,256]{1,0:T(8,128)(2,1)}, u32[]{:S(2)}, u32[]{:S(2)}) collective-permute-start(bf16[1024,256]{1,0:T(8,128)(2,1)S(1)} %get-tuple-element.38), channel_id=1, source_target_pairs={{0,16},{1,17},{2,18},{3,19},{4,20},{5,21},{6,22},{7,23},{16,0},{17... | collective-permute-start | bytes 1572872 | tf_op jit(solution)/shard_map/ppermute | solution.py:176
  31.4 5.4 %collective-permute-done.1 = bf16[640,256]{1,0:T(8,128)(2,1)} collective-permute-done((bf16[640,256]{1,0:T(8,128)(2,1)S(1)}, bf16[640,256]{1,0:T(8,128)(2,1)}, u32[]{:S(2)}, u32[]{:S(2)}) %collective-permute-start.1) | collective-permute-done | bytes 327712 | tf_op jit(solution)/shard_map/ppermute | solution.py:176
  36.7 2.6 %collective-permute-start.10 = (bf16[1024,256]{1,0:T(8,128)(2,1)S(1)}, bf16[1024,256]{1,0:T(8,128)(2,1)}, u32[]{:S(2)}, u32[]{:S(2)}) collective-permute-start(bf16[1024,256]{1,0:T(8,128)(2,1)S(1)} %get-tuple-element.39), channel_id=1, source_target_pairs={{0,17},{1,16},{2,19},{3,18},{4,21},{5,20},{6,23},{7,22},{16,1},{17... | collective-permute-start | bytes 1572872 | tf_op jit(solution)/shard_map/ppermute | solution.py:176
  40.0 4.6 %copy-done = bf16[1,1,1,2,6,2048,256]{6,5,4,3,2,1,0:T(8,128)(2,1)S(1)} copy-done((bf16[1,1,1,2,6,2048,256]{6,5,4,3,2,1,0:T(8,128)(2,1)S(1)}, bf16[1,1,1,2,6,2048,256]{6,5,4,3,2,1,0:T(8,128)(2,1)}, u32[]{:S(2)}) %copy-start) | copy-done | bytes 12582936
  44.6 9.9 %shard_map.87 = f32[6,8,128]{2,1,0:T(8,128)S(1)} custom-call(s32[1,6]{1,0:T(1,128)S(1)} %copy-done.2, bf16[6,8,128]{2,1,0:T(8,128)(2,1)S(1)} %bitcast.45, bf16[2,6,2048,256]{3,2,1,0:T(8,128)(2,1)S(1)} %bitcast.43, bf16[2,6,2048,256]{3,2,1,0:T(8,128)(2,1)S(1)} %bitcast.44), custom_call_target="tpu_custom_call" | custom-call | flops 100663296 | bytes 12582912 | tf_op jit(solution)/shard_map/pallas_call | solution.py:211
  54.6 4.6 %fusion = f32[2,6,4096]{2,1,0:T(8,128)S(1)} fusion(bf16[1,1,1,1024,4096]{4,3,2,1,0:T(8,128)(2,1)} %param.10, bf16[1,6,1024]{2,1,0:T(8,128)(2,1)S(1)} %get-tuple-element.47, bf16[1,6,1024]{2,1,0:T(8,128)(2,1)S(1)} %get-tuple-element.46), kind=kOutput, calls=%fused_computation | convolution fusion | flops 100675584 | bytes 8609792 | tf_op jit(solution)/shard_map/jrs,sd->jrd/dot_general | solution.py:238
  59.3 2.7 %collective-permute-start.2 = (f32[2,6,2048]{2,1,0:T(8,128)S(1)}, f32[2,6,2048]{2,1,0:T(8,128)S(1)}, u32[]{:S(2)}, u32[]{:S(2)}) collective-permute-start(f32[2,6,2048]{2,1,0:T(8,128)S(1)} %constant_dynamic-slice_fusion.2), channel_id=1, source_target_pairs={{0,4},{1,5},{2,6},{3,7},{4,0},{5,1},{6,2},{7,3},{8,12},{9,13},{10,... | collective-permute-start | bytes 294920 | tf_op jit(solution)/shard_map/ppermute | solution.py:25
  61.9 1.7 %bitcast_dynamic-update-slice_fusion.8 = bf16[1,1,1,2,4096,256]{5,4,3,2,1,0:T(8,128)(2,1)} fusion(bf16[1,1,1,2,4096,256]{5,4,3,2,1,0:T(8,128)(2,1)} %bitcast_dynamic-update-slice_fusion.9, s32[]{:T(128)S(6)} %select_n.110, bf16[512,256]{1,0:T(8,128)(2,1)} %collective-permute-done.6), kind=kLoop, calls=%fused_computation.10 | loop fusion | bytes 524292 | tf_op jit(solution)/shard_map/dynamic_update_slice | solution.py:287
  63.6 3.0 %collective-permute-done.2 = f32[2,6,2048]{2,1,0:T(8,128)S(1)} collective-permute-done((f32[2,6,2048]{2,1,0:T(8,128)S(1)}, f32[2,6,2048]{2,1,0:T(8,128)S(1)}, u32[]{:S(2)}, u32[]{:S(2)}) %collective-permute-start.2) | collective-permute-done | bytes 98336 | tf_op jit(solution)/shard_map/ppermute | solution.py:25
  66.6 0.8 collective-permute-start.3
  67.4 1.7 %bitcast_dynamic-update-slice_fusion.7 = bf16[1,1,1,2,4096,256]{5,4,3,2,1,0:T(8,128)(2,1)} fusion(bf16[1,1,1,2,4096,256]{5,4,3,2,1,0:T(8,128)(2,1)} %bitcast_dynamic-update-slice_fusion.8, s32[]{:T(128)S(6)} %select_n.109, bf16[640,256]{1,0:T(8,128)(2,1)} %collective-permute-done), kind=kLoop, calls=%fused_computation.9 | loop fusion | bytes 655364 | tf_op jit(solution)/shard_map/dynamic_update_slice | solution.py:287
  69.2 1.8 %collective-permute-done.3 = f32[2,6,1024]{2,1,0:T(8,128)S(1)} collective-permute-done((f32[2,6,1024]{2,1,0:T(8,128)S(1)}, f32[2,6,1024]{2,1,0:T(8,128)S(1)}, u32[]{:S(2)}, u32[]{:S(2)}) %collective-permute-start.3) | collective-permute-done | bytes 49184 | tf_op jit(solution)/shard_map/ppermute | solution.py:25
  71.6 1.7 %bitcast_dynamic-update-slice_fusion.6 = bf16[1,1,1,2,4096,256]{5,4,3,2,1,0:T(8,128)(2,1)} fusion(bf16[1,1,1,2,4096,256]{5,4,3,2,1,0:T(8,128)(2,1)} %bitcast_dynamic-update-slice_fusion.7, s32[]{:T(128)S(6)} %select_n.110, bf16[640,256]{1,0:T(8,128)(2,1)} %collective-permute-done.1), kind=kLoop, calls=%fused_computation.8 | loop fusion | bytes 655364 | tf_op jit(solution)/shard_map/dynamic_update_slice | solution.py:287
  73.3 8.8 %collective-permute-done.4 = f32[2,6,512]{2,1,0:T(8,128)S(1)} collective-permute-done((f32[2,6,512]{2,1,0:T(8,128)S(1)}, f32[2,6,512]{2,1,0:T(8,128)S(1)}, u32[]{:S(2)}, u32[]{:S(2)}) %collective-permute-start.4) | collective-permute-done | bytes 24608 | tf_op jit(solution)/shard_map/ppermute | solution.py:25
  82.1 1.0 %collective-permute-start.11 = (bf16[640,256]{1,0:T(8,128)(2,1)S(1)}, bf16[640,256]{1,0:T(8,128)(2,1)S(1)}, u32[]{:S(2)}, u32[]{:S(2)}) collective-permute-start(bf16[640,256]{1,0:T(8,128)(2,1)S(1)} %get-tuple-element.40), channel_id=1, source_target_pairs={{0,16},{1,17},{2,18},{3,19},{4,20},{5,21},{6,22},{7,23},{16,0},{17... | collective-permute-start | bytes 983048 | tf_op jit(solution)/shard_map/ppermute | solution.py:176
  83.7 1.9 %collective-permute-start.12 = (bf16[640,256]{1,0:T(8,128)(2,1)S(1)}, bf16[640,256]{1,0:T(8,128)(2,1)S(1)}, u32[]{:S(2)}, u32[]{:S(2)}) collective-permute-start(bf16[640,256]{1,0:T(8,128)(2,1)S(1)} %get-tuple-element.41), channel_id=1, source_target_pairs={{0,17},{1,16},{2,19},{3,18},{4,21},{5,20},{6,23},{7,22},{16,1},{17... | collective-permute-start | bytes 983048 | tf_op jit(solution)/shard_map/ppermute | solution.py:176
  85.6 1.9 %bitcast_dynamic-update-slice_fusion.1 = bf16[1,1,1,2,4096,256]{5,4,3,2,1,0:T(8,128)(2,1)} fusion(bf16[1,1,1,2,4096,256]{5,4,3,2,1,0:T(8,128)(2,1)} %bitcast_dynamic-update-slice_fusion.6, s32[]{:T(128)S(6)} %select_n.109, bf16[1152,256]{1,0:T(8,128)(2,1)} %collective-permute-done.7), kind=kLoop, calls=%fused_computation.3 | loop fusion | bytes 1179652 | tf_op jit(solution)/shard_map/dynamic_update_slice | solution.py:287
  87.5 1.9 %bitcast_dynamic-update-slice_fusion = bf16[1,1,1,2,4096,256]{5,4,3,2,1,0:T(8,128)(2,1)} fusion(bf16[1,1,1,2,4096,256]{5,4,3,2,1,0:T(8,128)(2,1)} %bitcast_dynamic-update-slice_fusion.1, s32[]{:T(128)S(6)} %select_n.110, bf16[1152,256]{1,0:T(8,128)(2,1)} %collective-permute-done.8), kind=kLoop, calls=%fused_computation.2 | loop fusion | bytes 1179652 | tf_op jit(solution)/shard_map/dynamic_update_slice | solution.py:287
  89.4 2.1 %collective-permute-start.14 = (bf16[128,256]{1,0:T(8,128)(2,1)S(1)}, bf16[128,256]{1,0:T(8,128)(2,1)S(1)}, u32[]{:S(2)}, u32[]{:S(2)}) collective-permute-start(bf16[128,256]{1,0:T(8,128)(2,1)S(1)} %copy-done.4), channel_id=1, source_target_pairs={{0,17},{1,16},{2,19},{3,18},{4,21},{5,20},{6,23},{7,22},{16,1},{17... | collective-permute-start | bytes 196616 | tf_op jit(solution)/shard_map/ppermute | solution.py:176
  91.5 1.9 %bitcast_dynamic-update-slice_fusion.3 = bf16[1,1,1,2,4096,256]{5,4,3,2,1,0:T(8,128)(2,1)} fusion(bf16[1,1,1,2,4096,256]{5,4,3,2,1,0:T(8,128)(2,1)} %bitcast_dynamic-update-slice_fusion, s32[]{:T(128)S(6)} %select_n.109, bf16[1024,256]{1,0:T(8,128)(2,1)} %collective-permute-done.9), kind=kLoop, calls=%fused_computation.5 | loop fusion | bytes 1048580 | tf_op jit(solution)/shard_map/dynamic_update_slice | solution.py:287
  93.4 1.9 %bitcast_dynamic-update-slice_fusion.2 = bf16[1,1,1,2,4096,256]{5,4,3,2,1,0:T(8,128)(2,1)} fusion(bf16[1,1,1,2,4096,256]{5,4,3,2,1,0:T(8,128)(2,1)} %bitcast_dynamic-update-slice_fusion.3, s32[]{:T(128)S(6)} %select_n.110, bf16[1024,256]{1,0:T(8,128)(2,1)} %collective-permute-done.10), kind=kLoop, calls=%fused_computation.4 | loop fusion | bytes 1048580 | tf_op jit(solution)/shard_map/dynamic_update_slice | solution.py:287
  95.3 0.7 bitcast_dynamic-update-slice_fusion.5
  96.0 2.4 %collective-permute-done.12 = bf16[640,256]{1,0:T(8,128)(2,1)S(1)} collective-permute-done((bf16[640,256]{1,0:T(8,128)(2,1)S(1)}, bf16[640,256]{1,0:T(8,128)(2,1)S(1)}, u32[]{:S(2)}, u32[]{:S(2)}) %collective-permute-start.12) | collective-permute-done | bytes 327712 | tf_op jit(solution)/shard_map/ppermute | solution.py:176
  (43 shorter events, 6.1 us)
Async XLA Ops:
  0.6 7.9 %copy-start.1 = (s32[1,1,1,256]{3,2,1,0:T(1,128)S(1)}, s32[1,1,1,256]{3,2,1,0:T(1,128)}, u32[]{:S(2)}) copy-start(s32[1,1,1,256]{3,2,1,0:T(1,128)} %param.12) | copy-start | bytes 3076
  3.4 19.4 %collective-permute-start.5 = (bf16[512,256]{1,0:T(8,128)(2,1)}, bf16[512,256]{1,0:T(8,128)(2,1)}, u32[]{:S(2)}, u32[]{:S(2)}) collective-permute-start(bf16[512,256]{1,0:T(8,128)(2,1)} %get-tuple-element.32), channel_id=1, source_target_pairs={{0,16},{1,17},{2,18},{3,19},{4,20},{5,21},{6,22},{7,23},{16,0},{17... | collective-permute-start | bytes 786440 | tf_op jit(solution)/shard_map/ppermute | solution.py:176
  6.4 52.9 %collective-permute-start.6 = (bf16[512,256]{1,0:T(8,128)(2,1)}, bf16[512,256]{1,0:T(8,128)(2,1)}, u32[]{:S(2)}, u32[]{:S(2)}) collective-permute-start(bf16[512,256]{1,0:T(8,128)(2,1)} %get-tuple-element.33), channel_id=1, source_target_pairs={{0,17},{1,16},{2,19},{3,18},{4,21},{5,20},{6,23},{7,22},{16,1},{17... | collective-permute-start | bytes 786440 | tf_op jit(solution)/shard_map/ppermute | solution.py:176
  8.5 31.5 %copy-start.2 = (s32[1,6]{1,0:T(1,128)S(1)}, s32[1,6]{1,0:T(1,128)}, u32[]{:S(2)}) copy-start(s32[1,6]{1,0:T(1,128)} %lengths_ref.1) | copy-start | bytes 76
  18.2 0.6 copy-start.3
  18.8 0.6 copy-start.5
  19.5 10.8 %collective-permute-start = (bf16[640,256]{1,0:T(8,128)(2,1)S(1)}, bf16[640,256]{1,0:T(8,128)(2,1)}, u32[]{:S(2)}, u32[]{:S(2)}) collective-permute-start(bf16[640,256]{1,0:T(8,128)(2,1)S(1)} %get-tuple-element.23), channel_id=1, source_target_pairs={{0,16},{1,17},{2,18},{3,19},{4,20},{5,21},{6,22},{7,23},{16,0},{17... | collective-permute-start | bytes 983048 | tf_op jit(solution)/shard_map/ppermute | solution.py:176
  20.6 16.1 %collective-permute-start.1 = (bf16[640,256]{1,0:T(8,128)(2,1)S(1)}, bf16[640,256]{1,0:T(8,128)(2,1)}, u32[]{:S(2)}, u32[]{:S(2)}) collective-permute-start(bf16[640,256]{1,0:T(8,128)(2,1)S(1)} %get-tuple-element.24), channel_id=1, source_target_pairs={{0,17},{1,16},{2,19},{3,18},{4,21},{5,20},{6,23},{7,22},{16,1},{17... | collective-permute-start | bytes 983048 | tf_op jit(solution)/shard_map/ppermute | solution.py:176
  21.0 62.8 %collective-permute-start.7 = (bf16[1152,256]{1,0:T(8,128)(2,1)S(1)}, bf16[1152,256]{1,0:T(8,128)(2,1)}, u32[]{:S(2)}, u32[]{:S(2)}) collective-permute-start(bf16[1152,256]{1,0:T(8,128)(2,1)S(1)} %get-tuple-element.36), channel_id=1, source_target_pairs={{0,16},{1,17},{2,18},{3,19},{4,20},{5,21},{6,22},{7,23},{16,0},{17... | collective-permute-start | bytes 1769480 | tf_op jit(solution)/shard_map/ppermute | solution.py:176
  22.7 64.8 %collective-permute-start.8 = (bf16[1152,256]{1,0:T(8,128)(2,1)S(1)}, bf16[1152,256]{1,0:T(8,128)(2,1)}, u32[]{:S(2)}, u32[]{:S(2)}) collective-permute-start(bf16[1152,256]{1,0:T(8,128)(2,1)S(1)} %get-tuple-element.37), channel_id=1, source_target_pairs={{0,17},{1,16},{2,19},{3,18},{4,21},{5,20},{6,23},{7,22},{16,1},{17... | collective-permute-start | bytes 1769480 | tf_op jit(solution)/shard_map/ppermute | solution.py:176
  30.2 59.2 %collective-permute-start.9 = (bf16[1024,256]{1,0:T(8,128)(2,1)S(1)}, bf16[1024,256]{1,0:T(8,128)(2,1)}, u32[]{:S(2)}, u32[]{:S(2)}) collective-permute-start(bf16[1024,256]{1,0:T(8,128)(2,1)S(1)} %get-tuple-element.38), channel_id=1, source_target_pairs={{0,16},{1,17},{2,18},{3,19},{4,20},{5,21},{6,22},{7,23},{16,0},{17... | collective-permute-start | bytes 1572872 | tf_op jit(solution)/shard_map/ppermute | solution.py:176
  36.7 56.7 %collective-permute-start.10 = (bf16[1024,256]{1,0:T(8,128)(2,1)S(1)}, bf16[1024,256]{1,0:T(8,128)(2,1)}, u32[]{:S(2)}, u32[]{:S(2)}) collective-permute-start(bf16[1024,256]{1,0:T(8,128)(2,1)S(1)} %get-tuple-element.39), channel_id=1, source_target_pairs={{0,17},{1,16},{2,19},{3,18},{4,21},{5,20},{6,23},{7,22},{16,1},{17... | collective-permute-start | bytes 1572872 | tf_op jit(solution)/shard_map/ppermute | solution.py:176
  40.0 4.6 %copy-start = (bf16[1,1,1,2,6,2048,256]{6,5,4,3,2,1,0:T(8,128)(2,1)S(1)}, bf16[1,1,1,2,6,2048,256]{6,5,4,3,2,1,0:T(8,128)(2,1)}, u32[]{:S(2)}) copy-start(bf16[1,1,1,2,6,2048,256]{6,5,4,3,2,1,0:T(8,128)(2,1)} %param.8) | copy-start | bytes 37748740
  59.2 28.3 %copy-start.6 = (bf16[128,256]{1,0:T(8,128)(2,1)S(1)}, bf16[128,256]{1,0:T(8,128)(2,1)}, u32[]{:S(2)}) copy-start(bf16[128,256]{1,0:T(8,128)(2,1)} %copy-done.5) | copy-start | bytes 196612
  59.2 30.2 %copy-start.4 = (bf16[128,256]{1,0:T(8,128)(2,1)S(1)}, bf16[128,256]{1,0:T(8,128)(2,1)}, u32[]{:S(2)}) copy-start(bf16[128,256]{1,0:T(8,128)(2,1)} %copy-done.3) | copy-start | bytes 196612
  59.3 7.3 %collective-permute-start.2 = (f32[2,6,2048]{2,1,0:T(8,128)S(1)}, f32[2,6,2048]{2,1,0:T(8,128)S(1)}, u32[]{:S(2)}, u32[]{:S(2)}) collective-permute-start(f32[2,6,2048]{2,1,0:T(8,128)S(1)} %constant_dynamic-slice_fusion.2), channel_id=1, source_target_pairs={{0,4},{1,5},{2,6},{3,7},{4,0},{5,1},{6,2},{7,3},{8,12},{9,13},{10,... | collective-permute-start | bytes 294920 | tf_op jit(solution)/shard_map/ppermute | solution.py:25
  66.6 4.3 %collective-permute-start.3 = (f32[2,6,1024]{2,1,0:T(8,128)S(1)}, f32[2,6,1024]{2,1,0:T(8,128)S(1)}, u32[]{:S(2)}, u32[]{:S(2)}) collective-permute-start(f32[2,6,1024]{2,1,0:T(8,128)S(1)} %constant_dynamic-slice_fusion.1), channel_id=1, source_target_pairs={{0,2},{1,3},{2,0},{3,1},{4,6},{5,7},{6,4},{7,5},{8,10},{9,11},{10,... | collective-permute-start | bytes 147464 | tf_op jit(solution)/shard_map/ppermute | solution.py:25
  71.0 11.1 %collective-permute-start.4 = (f32[2,6,512]{2,1,0:T(8,128)S(1)}, f32[2,6,512]{2,1,0:T(8,128)S(1)}, u32[]{:S(2)}, u32[]{:S(2)}) collective-permute-start(f32[2,6,512]{2,1,0:T(8,128)S(1)} %constant_dynamic-slice_fusion), channel_id=1, source_target_pairs={{0,1},{1,0},{2,3},{3,2},{4,5},{5,4},{6,7},{7,6},{8,9},{9,8},{10,11... | collective-permute-start | bytes 73736 | tf_op jit(solution)/shard_map/ppermute | solution.py:25
  82.1 13.2 %collective-permute-start.11 = (bf16[640,256]{1,0:T(8,128)(2,1)S(1)}, bf16[640,256]{1,0:T(8,128)(2,1)S(1)}, u32[]{:S(2)}, u32[]{:S(2)}) collective-permute-start(bf16[640,256]{1,0:T(8,128)(2,1)S(1)} %get-tuple-element.40), channel_id=1, source_target_pairs={{0,16},{1,17},{2,18},{3,19},{4,20},{5,21},{6,22},{7,23},{16,0},{17... | collective-permute-start | bytes 983048 | tf_op jit(solution)/shard_map/ppermute | solution.py:176
  83.7 14.7 %collective-permute-start.12 = (bf16[640,256]{1,0:T(8,128)(2,1)S(1)}, bf16[640,256]{1,0:T(8,128)(2,1)S(1)}, u32[]{:S(2)}, u32[]{:S(2)}) collective-permute-start(bf16[640,256]{1,0:T(8,128)(2,1)S(1)} %get-tuple-element.41), channel_id=1, source_target_pairs={{0,17},{1,16},{2,19},{3,18},{4,21},{5,20},{6,23},{7,22},{16,1},{17... | collective-permute-start | bytes 983048 | tf_op jit(solution)/shard_map/ppermute | solution.py:176
  87.5 11.8 %collective-permute-start.13 = (bf16[128,256]{1,0:T(8,128)(2,1)S(1)}, bf16[128,256]{1,0:T(8,128)(2,1)S(1)}, u32[]{:S(2)}, u32[]{:S(2)}) collective-permute-start(bf16[128,256]{1,0:T(8,128)(2,1)S(1)} %copy-done.6), channel_id=1, source_target_pairs={{0,16},{1,17},{2,18},{3,19},{4,20},{5,21},{6,22},{7,23},{16,0},{17... | collective-permute-start | bytes 196616 | tf_op jit(solution)/shard_map/ppermute | solution.py:176
  89.4 10.5 %collective-permute-start.14 = (bf16[128,256]{1,0:T(8,128)(2,1)S(1)}, bf16[128,256]{1,0:T(8,128)(2,1)S(1)}, u32[]{:S(2)}, u32[]{:S(2)}) collective-permute-start(bf16[128,256]{1,0:T(8,128)(2,1)S(1)} %copy-done.4), channel_id=1, source_target_pairs={{0,17},{1,16},{2,19},{3,18},{4,21},{5,20},{6,23},{7,22},{16,1},{17... | collective-permute-start | bytes 196616 | tf_op jit(solution)/shard_map/ppermute | solution.py:176
